TPU v7x, 32 devices: a whole 2x2x4 slice. The times are simulated.
32 devices in a mesh: epoch: 4 (over z), prow: 2 (over x), pcol: 4 (over y, core).
Axes of the slice: x: 2, y: 2, z: 4, core: 2. Of those that a mesh axis runs over, the one named last changes fastest.
Arguments:
- steps: int32 [2, 8192], P(None, 'epoch'), may hold values from 0 to 47
- harmonic: int32 [4096], replicated, may hold values from 0 to 4095, each once
- col_scale: float32 [4096], replicated, may hold values from 0.3 to 3
- taps: float32 [256], replicated, may hold values from -0.375 to 0.375
- ridge: float32 [4096], P(('epoch', 'prow')), may hold values from 0.1 to 1
Outputs:
- panel: float32 [4096, 256], P(('epoch', 'prow'))
- schur: float32 [4096, 4096], P(('epoch', 'prow'), 'pcol')
Inputs may be any that keep to these rules, and one draw needn't show every extreme that they name: `harmonic`: each of 0 to 4095 once.
All inputs are finite; a program needn't handle non-finite values.
Results may differ from a plain program's by a relative error of at most 0.0028.
Values may be sent and summed in bfloat16 or wider, within the bound.
No kernel may reach another device: no remote copies, remote signals or barrier semaphores. Data moves between devices by JAX's collectives and lax.ppermute only.
A program may use at most 128 MiB of HBM per device.

v0:
```python
import math

import jax
import jax.numpy as jnp
from jax import lax
from jax.sharding import PartitionSpec as P

B = 256


phase_count = 4096
angle_step = 2.0 * math.pi / 4096.0


def carried_in(value, axis, join, neutral):
    count, mine = (lax.axis_size(axis), lax.axis_index(axis))
    pieces = lax.all_gather(value, axis)
    total = jnp.full_like(value, 0) + jnp.asarray(neutral, value.dtype)

    def hop(position, total):
        longer = join(total, pieces[position])
        return jnp.where(position < mine, longer, total)

    return lax.fori_loop(0, count - 1, hop, total)


def shifted(x, axis, by):
    count = lax.axis_size(axis)
    pairs = [(i, i + by) for i in range(count) if 0 <= i + by < count]
    return lax.ppermute(x, axis, pairs)


def from_root(value, axis, source):
    kept = jnp.where(lax.axis_index(axis) == source, value, 0).astype(value.dtype)
    return lax.psum(kept, axis)


def toeplitz_pair(taps):
    count = taps.shape[0]
    pattern = jnp.concatenate(
        [jnp.zeros((1,), jnp.float32), taps[::-1], jnp.zeros((count,), jnp.float32)]
    )
    full = (
        jnp.tile(pattern, count)[: 2 * count * count].reshape(count, 2 * count).astype(jnp.bfloat16)
    )
    return (full[:, :count], full[:, count:])


def harmonic_design(phase_first, phase_second, orders, degrees, scales):
    indices = (
        phase_first[:, None] * orders[None, :] + phase_second[:, None] * degrees[None, :]
    ) % phase_count
    angle = indices.astype(jnp.float32) * angle_step
    return (jnp.cos(angle) + jnp.sin(angle)) * scales[None, :]


def add_phase(earlier, later):
    return (earlier + later) % phase_count


def on_device(steps, harmonic, col_scale, taps, ridge):
    epochs_here = steps.shape[1]
    count = taps.shape[0]
    params = harmonic.shape[0]
    n_epoch = lax.axis_size("epoch")
    n_row = lax.axis_size("prow")
    n_col = lax.axis_size("pcol")
    row_block = params // (n_epoch * n_row)
    col_block = params // n_col
    epoch_id = lax.axis_index("epoch")
    row_id = lax.axis_index("prow")
    col_id = lax.axis_index("pcol")
    row_harm = lax.dynamic_slice_in_dim(
        harmonic.reshape(n_epoch, n_row, row_block), row_id, 1, 1
    ).reshape(-1)
    row_scale = lax.dynamic_slice_in_dim(
        col_scale.reshape(n_epoch, n_row, row_block), row_id, 1, 1
    ).reshape(-1)
    col_harm = lax.dynamic_slice_in_dim(harmonic, col_id * col_block, col_block)
    col_scales = lax.dynamic_slice_in_dim(col_scale, col_id * col_block, col_block)
    harm = jnp.concatenate([row_harm, col_harm])
    scales = jnp.concatenate([row_scale, col_scales])
    orders = harm // 64
    degrees = harm % 64
    running = jnp.cumsum(steps, axis=1)
    totals = running[:, -1] % phase_count
    base = carried_in(totals, "epoch", add_phase, jnp.zeros((2,), jnp.int32))
    phase = (base[:, None] + running) % phase_count
    design = harmonic_design(phase[0], phase[1], orders, degrees, scales).astype(jnp.bfloat16)
    tail = shifted(design[epochs_here - count :], "epoch", 1)
    joined = jnp.concatenate([tail, design], axis=0)
    blocks = epochs_here // count
    width = harm.shape[0]
    earlier_rows = joined[:epochs_here].reshape(blocks, count, width)
    current_rows = joined[count:].reshape(blocks, count, width)
    lower_part, upper_part = toeplitz_pair(taps)
    filtered = jnp.einsum(
        "ij,bjc->bic", lower_part, earlier_rows, preferred_element_type=jnp.float32
    )
    filtered = filtered + jnp.einsum(
        "ij,bjc->bic", upper_part, current_rows, preferred_element_type=jnp.float32
    )
    filtered = filtered.reshape(epochs_here, width).astype(jnp.bfloat16)
    row_cols = filtered[:, : params // n_row]
    col_cols = filtered[:, params // n_row :]
    scale_total = 1.0 / (epochs_here * n_epoch)
    product = lax.dot_general(
        row_cols, col_cols, (((0,), (0,)), ((), ())), preferred_element_type=jnp.float32
    )
    normal = lax.psum_scatter(product * scale_total, "epoch", scatter_dimension=0, tiled=True)
    first_row = (epoch_id * n_row + row_id) * row_block
    global_rows = first_row + jnp.arange(row_block, dtype=jnp.int32)
    global_cols = col_id * col_block + jnp.arange(col_block, dtype=jnp.int32)
    normal = normal + jnp.where(
        global_rows[:, None] == global_cols[None, :], ridge[:, None], jnp.float32(0.0)
    )
    leading_cols = normal[:, :B]
    spread = from_root(leading_cols, "pcol", 0)
    gathered = lax.all_gather(spread, ("epoch", "prow"), axis=0, tiled=True)
    leading = jnp.linalg.cholesky(gathered[:B])
    solved = jax.scipy.linalg.solve_triangular(leading, gathered.T, lower=True).T
    own_rows = lax.dynamic_slice_in_dim(solved, first_row, row_block, 0)
    col_rows = lax.dynamic_slice_in_dim(solved, col_id * col_block, col_block, 0)
    schur = normal - jnp.dot(
        own_rows, col_rows.T, precision=lax.Precision.HIGHEST, preferred_element_type=jnp.float32
    )
    return (own_rows, schur)


def solution(mesh):
    in_specs = (P(None, "epoch"), P(), P(), P(), P(("epoch", "prow")))
    out_specs = (P(("epoch", "prow"), None), P(("epoch", "prow"), "pcol"))
    return jax.shard_map(
        on_device, mesh=mesh, in_specs=in_specs, out_specs=out_specs, check_vma=False
    )
```

profile of v0, /device:TPU:0, one launch (start us, length us, event | category | flops | bytes accessed | tf_op | source)
XLA Modules:
  0.0 628.4 jit_solution(15423884781415984185)
XLA Ops:
  7.2 0.7 reshape.259
  7.9 0.7 dynamic_slice.27
  9.3 0.7 reshape.260
  10.1 0.7 copy.42
  12.1 12.5 %all-gather = s32[4,1,2]{2,1,0:T(1,128)S(1)} all-gather(s32[1,1,2]{2,1,0:T(1,128)S(1)} %fusion.38), channel_id=1, replica_groups=mesh['epoch'=4,'prow'=2,'pcol'=4] {'epoch'}, dimensions={0}, use_global_device_ids=true | all-gather | bytes 40 | tf_op jit(solution)/shard_map/all_gather | solution.py:17
  24.9 103.6 %multiply_convert_fusion.1 = bf16[2048,3072]{1,0:T(8,128)(2,1)S(1)} fusion(f32[3072]{0:T(1024)S(1)} %pad_maximum_fusion.1, s32[3072]{0:T(1024)S(1)} %get-tuple-element.182, s32[2048]{0:T(1024)S(1)} %bitcast.88, s32[3072]{0:T(1024)S(1)} %get-tuple-element.181, s32[2048]{0:T(1024)S(1)} %bitcast.87), kind=kLoop, calls=%fused_computation.23 | loop fusion | flops 119537664 | bytes 12636160 | tf_op jit(solution)/shard_map/convert_element_type | solution.py:89
  128.6 4.6 copy-done
  133.2 2.4 collective-permute-start
  136.7 118.0 %fusion.7 = f32[8,3072,256]{1,2,0:T(8,128)} fusion(f32[3072]{0:T(1024)S(1)} %pad_maximum_fusion.1, s32[3072]{0:T(1024)S(1)} %get-tuple-element.182, s32[8,256]{1,0:T(8,128)S(1)} %mul.107, s32[3072]{0:T(1024)S(1)} %get-tuple-element.181, s32[8,256]{1,0:T(8,128)S(1)} %mul.103, bf16[256,256,1]{1,0,2:T(8,128)(2,1)S(1)} %slice_bitcast_fusion.11), kind=kOutput, calls=%fused_computation.24 | convolution fusion | flops 3340763136 | bytes 25350144 | tf_op jit(solution)/shard_map/ij,bjc->bic/dot_general | solution.py:100
  254.8 3.9 pad_maximum_fusion
  258.7 14.8 %add_convert_fusion = bf16[8,3072,256]{1,2,0:T(8,128)(2,1)} fusion(f32[8,3072,256]{1,2,0:T(8,128)} %fusion.7, bf16[8,256,3072]{2,1,0:T(8,128)(2,1)S(1)} %bitcast.77, bf16[256,512]{1,0:T(8,128)(2,1)S(1)} %convert_element_type.29), kind=kOutput, calls=%fused_computation.21 | convolution fusion | flops 3233808384 | bytes 50462720 | tf_op jit(solution)/shard_map/ij,bjc->bic/dot_general | solution.py:97
  273.6 14.6 %fusion.19 = f32[2048,1024]{0,1:T(8,128)} fusion(bf16[2048,3072]{1,0:T(8,128)(2,1)} %bitcast.78), kind=kOutput, calls=%fused_computation.42 | convolution fusion | flops 8592031744 | bytes 20971520 | tf_op jit(solution)/shard_map/dot_general | solution.py:107
  288.2 142.7 %reduce-scatter.2.cloned.1.call-done = f32[512,1024]{0,1:T(8,128)} async-done(((f32[2048,1024]{0,1:T(8,128)}), f32[512,1024]{0,1:T(8,128)}) %reduce-scatter.2.cloned.1.call-update) | async-done | bytes 2097168 | tf_op jit(solution)/shard_map/reduce_scatter | solution.py:110
  431.0 1.9 select_add_fusion
  432.9 0.8 slice_select_fusion
  433.8 34.1 %all-reduce.3.cloned.1.call-done = f32[512,256]{0,1:T(8,128)} async-done(((f32[512,256]{0,1:T(8,128)}), f32[512,256]{0,1:T(8,128)}) %all-reduce.3.cloned.1.call-update) | async-done | bytes 524304 | tf_op jit(solution)/shard_map/psum | solution.py:35
  467.9 75.6 %all-gather.3.cloned.1.call-done = f32[4096,256]{0,1:T(8,128)} async-done(((f32[512,256]{0,1:T(8,128)}), f32[4096,256]{0,1:T(8,128)}) %all-gather.3.cloned.1.call-update) | async-done | bytes 4194320 | tf_op jit(solution)/shard_map/all_gather | solution.py:119
  543.4 1.0 slice.126
  544.6 1.0 fusion.28
  545.6 11.7 %cholesky.50 = f32[128,128]{1,0:T(8,128)S(1)} custom-call(f32[128,128]{1,0:T(8,128)S(1)} %cholesky.118), custom_call_target="Cholesky" | custom-call | tf_op jit(solution)/shard_map/jit(cholesky)/cholesky | solution.py:120
  557.3 9.8 %custom-call.15 = f32[1,128,128]{1,2,0:T(8,128)S(1)} custom-call(f32[1,128,128]{2,1,0:T(8,128)S(1)} %get-tuple-element.178), custom_call_target="InvertDiagBlocksLowerTriangular" | custom-call | tf_op jit(solution)/shard_map/jit(cholesky)/cholesky | solution.py:120
  567.6 11.7 %cholesky.105 = f32[128,128]{1,0:T(8,128)S(1)} custom-call(f32[128,128]{1,0:T(8,128)S(1)} %convolution_subtract_fusion.2), custom_call_target="Cholesky" | custom-call | tf_op jit(solution)/shard_map/jit(cholesky)/cholesky | solution.py:120
  581.4 4.1 while.17
  582.2 1.4 bitcast_dynamic-update-slice_fusion.2
  584.2 1.4 bitcast_dynamic-update-slice_fusion.2
  585.5 19.7 %custom-call.16 = f32[2,128,128]{1,2,0:T(8,128)S(1)} custom-call(f32[2,128,128]{2,1,0:T(8,128)S(1)} %get-tuple-element.121), custom_call_target="InvertDiagBlocksLowerTriangular" | custom-call | tf_op jit(solution)/shard_map/jit(_solve_triangular)/triangular_solve | solution.py:121
  605.2 3.5 fusion.23
  608.7 3.5 convolution_subtract_fusion
  612.3 1.9 fusion.30
  614.2 3.3 convolution_subtract_fusion.1
  617.6 2.9 copy.30
  620.5 1.0 copy.29
  (64 shorter events, 6.3 us)
Async XLA Ops:
  7.2 423.8 %reduce-scatter.2.cloned.1.call-start = ((), (), s32[]{:S(2)}) async-start(), calls=%async_computation.1 | async-start | bytes 10485760 | tf_op jit(solution)/shard_map/reduce_scatter | solution.py:110
  24.9 110.8 %copy-start.3 = (f32[256]{0:T(256)S(1)}, f32[256]{0:T(256)}, u32[]{:S(2)}) copy-start(f32[256]{0:T(256)} %param.10) | copy-start | bytes 3076
  128.5 4.6 copy-start
  133.2 121.6 %collective-permute-start = (bf16[256,3072]{1,0:T(8,128)(2,1)S(1)}, bf16[256,3072]{1,0:T(8,128)(2,1)}, u32[]{:S(2)}, u32[]{:S(2)}) collective-permute-start(bf16[256,3072]{1,0:T(8,128)(2,1)S(1)} %slice.121), channel_id=1, source_target_pairs={{0,8},{8,16},{16,24},{1,9},{9,17},{17,25},{2,10},{10,18},{18,26},{... | collective-permute-start | bytes 4718600 | tf_op jit(solution)/shard_map/ppermute | solution.py:30
  136.7 118.1 %copy-start.1 = (bf16[2048,3072]{1,0:T(8,128)(2,1)S(1)}, bf16[2048,3072]{1,0:T(8,128)(2,1)}, u32[]{:S(2)}) copy-start(bf16[2048,3072]{1,0:T(8,128)(2,1)} %copy-done) | copy-start | bytes 37748740
  273.6 157.4 %copy-start.2 = (f32[512]{0:T(512)S(1)}, f32[512]{0:T(512)}, u32[]{:S(2)}) copy-start(f32[512]{0:T(512)} %param.11) | copy-start | bytes 6148
  288.2 179.7 %all-reduce.3.cloned.1.call-start = ((), (), s32[]{:S(2)}) async-start(), calls=%async_computation.2 | async-start | bytes 1048576 | tf_op jit(solution)/shard_map/psum | solution.py:35
  433.7 109.7 %all-gather.3.cloned.1.call-start = ((), (), s32[]{:S(2)}) async-start(), calls=%async_computation.3 | async-start | bytes 4718592 | tf_op jit(solution)/shard_map/all_gather | solution.py:119
Sparse Core Ops, SparseCore 0:
  288.3 142.6 reduce-scatter.1
  433.9 33.8 all-reduce.2
  470.0 73.3 all-gather.2
where the time goes:
time: 635 us; the launch traced here: 628 us
  waiting for transfers between devices  252 us (40%)
  other arithmetic  166 us (26%)
  matrix products  160 us (25%)
  local copies, waits for them, and re-layouts  18.6 us (3%)
  between operations  15.7 us (2%)
  blocking collectives  12.5 us (2%)
    reduce_scatter x1, waiting for transfers between devices, on_device(): lax.psum_scatter(product * scale_total, 'epoch', scatter_dimension=0, til...  143 us
    dot_general x1, matrix products, on_device(): jnp.einsum('ij,bjc->bic', upper_part, current_rows, preferred_element_typ...  118 us
    convert_element_type x1, other arithmetic, on_device(): harmonic_design(phase[0], phase[1], orders, degrees, scales)  104 us
    all_gather x1, waiting for transfers between devices, on_device(): gathered = lax.all_gather(spread, ('epoch', 'prow'), axis=0, tiled=True)  75.6 us
    psum x1, waiting for transfers between devices, from_root(): return lax.psum(kept, axis)  34.1 us
    another operation x6, other arithmetic, on_device(): leading = jnp.linalg.cholesky(gathered[:B])  34 us
    another operation x3, other arithmetic, on_device(): jax.scipy.linalg.solve_triangular(leading, gathered.T, lower=True)  19.7 us
    dot_general x1, matrix products, on_device(): jnp.einsum('ij,bjc->bic', lower_part, earlier_rows, preferred_element_typ...  14.8 us
  transfers between devices with their start and end apart: 4, of which 3 were waited for; matrix products, arithmetic and copies ran while one was open for 19% of the time, Pallas kernels for 0%

commit v1 on v0

v1 whole, which is shorter than its diff:
```python
import functools
import math

import jax
import jax.numpy as jnp
from jax import lax
from jax.experimental import pallas as pl
from jax.experimental.pallas import tpu as pltpu
from jax.sharding import PartitionSpec as P

B = 256

phase_count = 4096
SINE = (6.2831640442776635, -41.337142367123384, 81.34076873476997, -70.99343163979194)


def rotated(x, axis):
    count = lax.axis_size(axis)
    shifts = [[(i, (i + k) % count) for i in range(count)] for k in range(1, count)]
    return [x] + [lax.ppermute(x, axis, pairs) for pairs in shifts]


def gathered_doubling(x, axes):
    count, mine = lax.axis_size(axes), lax.axis_index(axes)
    size, held, have = x.shape[0], x, 1
    while have < count:
        take = min(have, count - have)
        pairs = [((i + have) % count, i) for i in range(count)]
        held = jnp.concatenate([held, lax.ppermute(held[: take * size], axes, pairs)])
        have += take
    return jnp.roll(held, mine * size)


def toeplitz_transposed(taps):
    count = taps.shape[0]
    pattern = jnp.concatenate(
        [jnp.zeros((1,), jnp.float32), taps[::-1], jnp.zeros((count,), jnp.float32)]
    )
    full = (
        jnp.tile(pattern, count)[: 2 * count * count].reshape(count, 2 * count).astype(jnp.bfloat16)
    )
    return full.T


def pick_chunk(width):
    for size in (256, 224, 192, 160, 128, 96, 64, 48, 32, 16):
        if width % size == 0:
            return size
    return width


def split3(x):
    high = x.astype(jnp.bfloat16)
    rest = x - high.astype(jnp.float32)
    mid = rest.astype(jnp.bfloat16)
    return high, mid, (rest - mid.astype(jnp.float32)).astype(jnp.bfloat16)


def dot_f32(a, b, b_dim):
    ah, am, al = split3(a)
    bh, bm, bl = split3(b)
    return lax.dot_general(
        jnp.concatenate([ah, ah, am, ah, al, am], axis=1),
        jnp.concatenate([bh, bm, bh, bl, bh, bm], axis=b_dim),
        (((1,), (b_dim,)), ((), ())),
        preferred_element_type=jnp.float32,
    )


def factor_panel(t, size, group):
    row = lax.broadcasted_iota(jnp.int32, t.shape, 0)
    for j in range(0, size, group):
        span = range(group)
        cols = [jnp.broadcast_to(t[:, j + k : j + k + 1], t.shape) for k in span]
        rows = [t[j + k : j + k + 1, :] for k in span]
        pivot = [[cols[l][j + k : j + k + 1, :] for l in span] for k in span]
        done = []
        for k in span:
            root = lax.rsqrt(pivot[k][k])
            inverse = root * root
            weight = rows[k] * inverse
            for l in range(k + 1, group):
                lower = pivot[l][k]
                rows[l] = rows[l] - lower * weight
                cols[l] = cols[l] - cols[k] * (pivot[k][l] * inverse)
                for q in range(k + 1, group):
                    pivot[l][q] = pivot[l][q] - lower * (pivot[k][q] * inverse)
            t = t - jnp.where(row >= j + group, cols[k], 0.0) * weight
            done.append(rows[k] * root)
        for k in span:
            t = jnp.where(row == j + k, done[k], t)
    return t


def invert_factor(m_ref, size, group):
    n = m_ref.shape[0]

    @pl.loop(0, n // size)
    def _(k):
        here = pl.ds(pl.multiple_of(k * size, size), size)
        panel = m_ref[here, :]
        lane = lax.broadcasted_iota(jnp.int32, (size, 2 * size), 1)
        row = lax.broadcasted_iota(jnp.int32, (size, 2 * size), 0)
        eye = jnp.where(lane == row, 1.0, 0.0)
        t = jnp.where(
            lane < size, panel[:, : 2 * size], jnp.where(lane - size == row, 1.0, 0.0)
        )
        t = factor_panel(t, size, group)
        inverse = pltpu.roll(t, size, 1)[:, :size]
        first = jnp.where(lane < size, eye, panel[:, : 2 * size])
        done = dot_f32(inverse, jnp.concatenate([first, panel[:, 2 * size :]], axis=1), 0)
        full = m_ref[...]
        below = lax.broadcasted_iota(jnp.int32, (n, size), 0) >= (k + 1) * size
        low = jnp.where(below, dot_f32(full[:, :size], inverse, 1), 0.0)
        kept = jnp.where(lax.broadcasted_iota(jnp.int32, (n, n), 1) < size, 0.0, full)
        m_ref[...] = pltpu.roll(kept - dot_f32(low, done, 0), n - size, 1)
        m_ref[here, :] = pltpu.roll(done, n - size, 1)


def fill_phases(mine, steps_refs, sums_ref, pt_ref):
    here = steps_refs[0].shape[1]
    blocks = here // 128
    count = len(steps_refs)
    for k, ref in enumerate(steps_refs):
        group = lax.rem(mine - k + count, count)
        for b in range(blocks):
            row = pl.multiple_of((group * blocks + b) * 2, 2)
            sums_ref[pl.ds(row, 2), :] = ref[:, b * 128 : (b + 1) * 128].astype(jnp.float32)
    total = sums_ref.shape[0]
    terms = sums_ref[...].astype(jnp.bfloat16)
    i = lax.broadcasted_iota(jnp.int32, (128, 128), 0)
    j = lax.broadcasted_iota(jnp.int32, (128, 128), 1)
    inside = jnp.dot(
        terms, jnp.where(i <= j, 1.0, 0.0).astype(jnp.bfloat16), preferred_element_type=jnp.float32
    )
    ends = jnp.dot(terms, jnp.ones((128, 128), jnp.bfloat16), preferred_element_type=jnp.float32)
    ends = ends.astype(jnp.int32)
    i = lax.broadcasted_iota(jnp.int32, (total, total), 0)
    j = lax.broadcasted_iota(jnp.int32, (total, total), 1)
    earlier = jnp.where((j < i) & ((i - j) % 2 == 0), 1.0, 0.0).astype(jnp.bfloat16)

    def before(x):
        return jnp.dot(
            earlier, x.astype(jnp.float32).astype(jnp.bfloat16), preferred_element_type=jnp.float32
        ).astype(jnp.int32)

    phase = inside.astype(jnp.int32) + before(ends & 127) + before(ends >> 7) * 128
    phase = phase & (phase_count - 1)
    high = (phase & 4032).astype(jnp.float32) * (1.0 / phase_count)
    low = (phase & 63).astype(jnp.float32) * (1.0 / phase_count)
    pt_ref[...] = jnp.zeros_like(pt_ref)
    pt_ref[4:5, :] = jnp.full((1, pt_ref.shape[1]), -0.125, jnp.float32)
    for b in range(total // 2):
        pt_ref[0:2, b * 128 : (b + 1) * 128] = high[2 * b : 2 * b + 2, :]
        pt_ref[2:4, b * 128 : (b + 1) * 128] = low[2 * b : 2 * b + 2, :]


def normal_kernel(shape, chunk, n_steps, *refs):
    rows, lead, cols, n_row = shape
    steps_refs = refs[:n_steps]
    params_ref, wt_ref, panel_ref, schur_ref = refs[n_steps : n_steps + 4]
    d_ref, f_ref, acc_ref, sums_ref, pt_ref, h_ref, m_ref = refs[n_steps + 4 :]
    width, tile = f_ref.shape
    count = wt_ref.shape[1]
    step = pl.program_id(0)
    total = pl.num_programs(0) * tile

    @pl.when(step == 0)
    def _():
        fill_phases(lax.axis_index("epoch"), steps_refs, sums_ref, pt_ref)
        h_ref[...] = jnp.concatenate(
            [params_ref[...], jnp.zeros((120, params_ref.shape[1]), jnp.float32)]
        ).T
        d_ref[:, :count] = jnp.zeros((width, count), jnp.bfloat16)
        acc_ref[...] = jnp.zeros_like(acc_ref)

    @pl.when(step > 0)
    def _():
        d_ref[:, :count] = d_ref[:, tile:]

    pt = pt_ref[:, pl.ds(pl.multiple_of(step * tile, tile), tile)].astype(jnp.bfloat16)

    @pl.loop(0, width // chunk)
    def _(part):
        here = pl.ds(pl.multiple_of(part * chunk, chunk), chunk)
        h = h_ref[here, :]
        turns = jnp.dot(h[:, :16].astype(jnp.bfloat16), pt, preferred_element_type=jnp.float32)
        turns = turns - jnp.round(turns)
        s = 0.25 - jnp.abs(turns)
        z = s * s
        poly = SINE[0] + z * (SINE[1] + z * (SINE[2] + z * SINE[3]))
        d_ref[here, count:] = ((s * poly) * h[:, 5:6]).astype(jnp.bfloat16)
        for b in range(tile // count):
            f_ref[here, b * count : (b + 1) * count] = jnp.dot(
                d_ref[here, b * count : (b + 2) * count],
                wt_ref[...],
                preferred_element_type=jnp.float32,
            ).astype(jnp.bfloat16)

    acc_ref[...] += lax.dot_general(
        f_ref[: rows + lead, :],
        f_ref[rows:, :],
        (((1,), (1,)), ((), ())),
        preferred_element_type=jnp.float32,
    )

    @pl.when(step == pl.num_programs(0) - 1)
    def _():
        first_row = (lax.axis_index("epoch") * n_row + lax.axis_index("prow")) * rows
        first_col = lax.axis_index("pcol") * cols
        i = lax.broadcasted_iota(jnp.int32, acc_ref.shape, 0)
        j = lax.broadcasted_iota(jnp.int32, acc_ref.shape, 1)
        i = jnp.where(i < rows, i + first_row, i - rows)
        j = jnp.where(j < lead, j, j - lead + first_col)
        acc_ref[...] = acc_ref[...] * (1.0 / total) + jnp.where(
            i == j, h_ref[: rows + lead, 6:7], 0.0
        )
        m_ref[...] = acc_ref[rows:, :lead]
        invert_factor(m_ref, 64, 8)
        i = lax.broadcasted_iota(jnp.int32, (lead, lead), 0)
        j = lax.broadcasted_iota(jnp.int32, (lead, lead), 1)
        inverse = jnp.where(i >= j, m_ref[...], 0.0)
        highest = functools.partial(
            lax.dot_general, precision=lax.Precision.HIGHEST, preferred_element_type=jnp.float32
        )
        panel_ref[...] = highest(acc_ref[:rows, :lead], inverse, (((1,), (1,)), ((), ())))
        for c in range(0, cols, 256):
            solved = highest(inverse, acc_ref[rows:, lead + c : lead + c + 256], (((1,), (0,)), ((), ())))
            schur_ref[:, c : c + 256] = acc_ref[:rows, lead + c : lead + c + 256] - highest(
                panel_ref[...], solved, (((1,), (0,)), ((), ()))
            )


def on_device(steps, harmonic, col_scale, taps, ridge):
    params = harmonic.shape[0]
    n_epoch = lax.axis_size("epoch")
    n_row = lax.axis_size("prow")
    n_col = lax.axis_size("pcol")
    rows = params // (n_epoch * n_row)
    cols = params // n_col
    first_row = (lax.axis_index("epoch") * n_row + lax.axis_index("prow")) * rows
    first_col = lax.axis_index("pcol") * cols
    steps_parts = rotated(steps, "epoch")
    ridge_lead = gathered_doubling(ridge, ("epoch", "prow"))[:B]
    width = rows + B + cols
    padded = -(-width // 128) * 128
    epochs = steps.shape[1] * n_epoch
    count = taps.shape[0]
    tile = 1024 if epochs % 1024 == 0 else count

    def own(x):
        return jnp.concatenate(
            [
                lax.dynamic_slice_in_dim(x, first_row, rows),
                x[:B],
                lax.dynamic_slice_in_dim(x, first_col, cols),
                jnp.zeros((padded - width,), x.dtype),
            ]
        )

    harm = own(harmonic)
    orders = (harm // 64).astype(jnp.float32)
    degrees = (harm % 64).astype(jnp.float32)
    ones = jnp.ones_like(orders)
    ridge_rows = jnp.concatenate([ridge, ridge_lead, jnp.zeros((padded - rows - B,), jnp.float32)])
    table = jnp.stack(
        [orders, degrees, orders, degrees, ones, own(col_scale) * math.sqrt(2.0), ridge_rows, 0 * ones]
    )
    whole = lambda i: (0, 0)
    vmem = lambda x: pl.BlockSpec(x.shape, whole)
    operands = (*steps_parts, table, toeplitz_transposed(taps))
    return pl.pallas_call(
        functools.partial(normal_kernel, (rows, B, cols, n_row), pick_chunk(width), len(steps_parts)),
        grid=(epochs // tile,),
        out_shape=(
            jax.ShapeDtypeStruct((rows, B), jnp.float32),
            jax.ShapeDtypeStruct((rows, cols), jnp.float32),
        ),
        in_specs=[vmem(x) for x in operands],
        out_specs=(pl.BlockSpec((rows, B), whole), pl.BlockSpec((rows, cols), whole)),
        scratch_shapes=[
            pltpu.VMEM((width, count + tile), jnp.bfloat16),
            pltpu.VMEM((width, tile), jnp.bfloat16),
            pltpu.VMEM((rows + B, B + cols), jnp.float32),
            pltpu.VMEM((2 * epochs // 128, 128), jnp.float32),
            pltpu.VMEM((16, epochs), jnp.float32),
            pltpu.VMEM((padded, 128), jnp.float32),
            pltpu.VMEM((B, B), jnp.float32),
        ],
        compiler_params=pltpu.CompilerParams(vmem_limit_bytes=56 * 1024 * 1024),
    )(*operands)


def solution(mesh):
    in_specs = (P(None, "epoch"), P(), P(), P(), P(("epoch", "prow")))
    out_specs = (P(("epoch", "prow"), None), P(("epoch", "prow"), "pcol"))
    return jax.shard_map(
        on_device, mesh=mesh, in_specs=in_specs, out_specs=out_specs, check_vma=False
    )
```

time: 635 us -> 112 us (0.18)
  waiting for transfers between devices: 252 us -> 6.25 us
  other arithmetic: 166 us -> 0.18 us
  matrix products: 160 us -> 0 us
  Pallas kernels: 0 us -> 84.5 us
  between operations: 15.7 us -> 0.76 us
  blocking collectives: 12.5 us -> 0 us
  local copies, waits for them, and re-layouts: 18.6 us -> 8.83 us
  starting transfers between devices: 2.56 us -> 10.8 us
    dot_general x4 -> x0, matrix products: 151 us -> none  [the longest x1 118 us: on_device(): jnp.einsum('ij,bjc->bic', upper_part, current_rows, preferred_element_typ...]
    reduce_scatter x1 -> x0, waiting for transfers between devices: 143 us -> none  [on_device(): lax.psum_scatter(product * scale_total, 'epoch', scatter_dimension=0, til...]
    convert_element_type x1 -> x2, other arithmetic: 104 us -> 0.06 us  [the longest x1 0.04 us: on_device(): orders = (harm // 64).astype(jnp.float32)]
    pallas_call x0 -> x1, Pallas kernels: none -> 84.5 us  [on_device(): pl.pallas_call(functools.partial(normal_kernel, (rows, B, cols, n_row), p...]
    all_gather x1 -> x0, waiting for transfers between devices: 75.6 us -> none  [on_device(): gathered = lax.all_gather(spread, ('epoch', 'prow'), axis=0, tiled=True)]
    another operation x12 -> x1, other arithmetic: 54.5 us -> 0.08 us  [the longest x6 34 us: on_device(): leading = jnp.linalg.cholesky(gathered[:B])]
    psum x1 -> x0, waiting for transfers between devices: 34.1 us -> none  [from_root(): return lax.psum(kept, axis)]
    all_gather x1 -> x0, blocking collectives: 12.5 us -> none  [carried_in(): pieces = lax.all_gather(value, axis)]
  transfers between devices with their start and end apart: 4 -> 6, of which waited for: 3 -> 2; matrix products, arithmetic and copies ran while one was open for 19% -> 8% of each run, Pallas kernels for 0% -> 0%
where the time goes in v1:
time: 112 us; the launch traced here: 111 us
  Pallas kernels  84.5 us (75%)
  starting transfers between devices  10.8 us (10%)
  local copies, waits for them, and re-layouts  8.83 us (8%)
  waiting for transfers between devices  6.25 us (6%)
    pallas_call x1, Pallas kernels, on_device(): pl.pallas_call(functools.partial(normal_kernel, (rows, B, cols, n_row), p...  84.5 us
    ppermute x3, starting transfers between devices, rotated(): return [x] + [lax.ppermute(x, axis, pairs) for pairs in shifts]  7.93 us
    ppermute x3, waiting for transfers between devices, gathered_doubling(): lax.ppermute(held[:take * size], axes, pairs)  6.24 us
    ppermute x3, starting transfers between devices, gathered_doubling(): lax.ppermute(held[:take * size], axes, pairs)  2.89 us
  transfers between devices with their start and end apart: 6, of which 2 were waited for; matrix products, arithmetic and copies ran while one was open for 8% of the time, Pallas kernels for 0%

profile of v1, /device:TPU:0, one launch (start us, length us, event | category | flops | bytes accessed | tf_op | source)
XLA Modules:
  0.0 111.4 jit_solution(16882360701610821972)
XLA Ops:
  0.6 0.0 copy-start
  0.6 4.1 %collective-permute-start.1 = (s32[2,2048]{1,0:T(2,128)}, s32[2,2048]{1,0:T(2,128)S(1)}, u32[]{:S(2)}, u32[]{:S(2)}) collective-permute-start(s32[2,2048]{1,0:T(2,128)} %refs_0_.1), channel_id=1, source_target_pairs={{0,16},{8,24},{16,0},{24,8},{1,17},{9,25},{17,1},{25,9},{2,18},{10... | collective-permute-start | bytes 49160 | tf_op jit(solution)/shard_map/ppermute | solution.py:20
  4.7 1.6 %collective-permute-start = (s32[2,2048]{1,0:T(2,128)}, s32[2,2048]{1,0:T(2,128)S(1)}, u32[]{:S(2)}, u32[]{:S(2)}) collective-permute-start(s32[2,2048]{1,0:T(2,128)} %refs_0_.1), channel_id=1, source_target_pairs={{0,8},{8,16},{16,24},{24,0},{1,9},{9,17},{17,25},{25,1},{2,10},{10... | collective-permute-start | bytes 49160 | tf_op jit(solution)/shard_map/ppermute | solution.py:20
  6.3 2.2 %collective-permute-start.2 = (s32[2,2048]{1,0:T(2,128)}, s32[2,2048]{1,0:T(2,128)S(1)}, u32[]{:S(2)}, u32[]{:S(2)}) collective-permute-start(s32[2,2048]{1,0:T(2,128)} %refs_0_.1), channel_id=1, source_target_pairs={{0,24},{8,0},{16,8},{24,16},{1,25},{9,1},{17,9},{25,17},{2,26},{10... | collective-permute-start | bytes 49160 | tf_op jit(solution)/shard_map/ppermute | solution.py:20
  8.6 0.9 collective-permute-start.3
  9.5 0.7 slice.13
  10.2 0.7 slice.14
  10.9 0.8 dynamic_slice.16
  11.6 0.8 dynamic_slice.18
  12.4 0.7 dynamic_slice.17
  13.1 0.7 dynamic_slice.19
  13.8 0.8 rev.3
  14.6 0.7 constant_dynamic-update-slice_fusion.7
  15.3 0.1 maximum_convert_fusion
  15.4 0.6 tile.11
  16.1 0.2 convert_element_type.26
  16.2 0.9 copy.7
  17.1 0.0 collective-permute-done.3
  17.1 0.7 collective-permute-start.4
  17.8 2.9 %collective-permute-done.4 = f32[1024]{0:T(1024)S(1)} collective-permute-done((f32[1024]{0:T(1024)S(1)}, f32[1024]{0:T(1024)S(1)}, u32[]{:S(2)}, u32[]{:S(2)}) %collective-permute-start.4) | collective-permute-done | bytes 4128 | tf_op jit(solution)/shard_map/ppermute | solution.py:29
  20.8 1.2 %collective-permute-start.5 = (f32[2048]{0:T(1024)S(1)}, f32[2048]{0:T(1024)S(1)}, u32[]{:S(2)}, u32[]{:S(2)}) collective-permute-start(f32[2048]{0:T(1024)S(1)} %pad_maximum_fusion), channel_id=1, source_target_pairs={{16,0},{20,4},{24,8},{28,12},{0,16},{4,20},{8,24},{12,28},{17,1},{... | collective-permute-start | bytes 24584 | tf_op jit(solution)/shard_map/ppermute | solution.py:29
  22.0 3.3 %collective-permute-done.5 = f32[2048]{0:T(1024)S(1)} collective-permute-done((f32[2048]{0:T(1024)S(1)}, f32[2048]{0:T(1024)S(1)}, u32[]{:S(2)}, u32[]{:S(2)}) %collective-permute-start.5) | collective-permute-done | bytes 8224 | tf_op jit(solution)/shard_map/ppermute | solution.py:29
  25.4 0.1 dynamic-slice
  25.5 0.7 stack.16.refs_4_
  26.2 0.0 collective-permute-done.1.refs_2_
  26.2 0.0 collective-permute-done.refs_1_
  26.2 0.0 collective-permute-done.2.refs_3_
  26.2 0.0 copy-start.3
  26.2 0.6 copy-done.1
  26.8 0.0 copy-done.2
  26.8 0.0 copy-done.3
  26.8 84.5 %shard_map.68 = (f32[512,256]{1,0:T(8,128)}, f32[512,1024]{1,0:T(8,128)}) custom-call(s32[2,2048]{1,0:T(2,128)} %refs_0_.1, s32[2,2048]{1,0:T(2,128)} %copy-done.2, s32[2,2048]{1,0:T(2,128)} %copy-done.1, s32[2,2048]{1,0:T(2,128)} %copy-done.3, f32[8,1792]{1,0:T(8,128)} %stack.16.refs_4_, bf16[512,256]{1,0:T(8,128)(2,1)} %bitcast.7), custom_call_target="tpu_custom_call" | custom-call | tf_op jit(solution)/shard_map/pallas_call | solution.py:272
  (24 shorter events, 0.2 us)
Async XLA Ops:
  0.6 16.5 %copy-start = (f32[512]{0:T(512)S(1)}, f32[512]{0:T(512)}, u32[]{:S(2)}) copy-start(f32[512]{0:T(512)} %param.9) | copy-start | bytes 6148
  0.6 25.6 %collective-permute-start.1 = (s32[2,2048]{1,0:T(2,128)}, s32[2,2048]{1,0:T(2,128)S(1)}, u32[]{:S(2)}, u32[]{:S(2)}) collective-permute-start(s32[2,2048]{1,0:T(2,128)} %refs_0_.1), channel_id=1, source_target_pairs={{0,16},{8,24},{16,0},{24,8},{1,17},{9,25},{17,1},{25,9},{2,18},{10... | collective-permute-start | bytes 49160 | tf_op jit(solution)/shard_map/ppermute | solution.py:20
  4.7 21.5 %collective-permute-start = (s32[2,2048]{1,0:T(2,128)}, s32[2,2048]{1,0:T(2,128)S(1)}, u32[]{:S(2)}, u32[]{:S(2)}) collective-permute-start(s32[2,2048]{1,0:T(2,128)} %refs_0_.1), channel_id=1, source_target_pairs={{0,8},{8,16},{16,24},{24,0},{1,9},{9,17},{17,25},{25,1},{2,10},{10... | collective-permute-start | bytes 49160 | tf_op jit(solution)/shard_map/ppermute | solution.py:20
  6.3 19.9 %collective-permute-start.2 = (s32[2,2048]{1,0:T(2,128)}, s32[2,2048]{1,0:T(2,128)S(1)}, u32[]{:S(2)}, u32[]{:S(2)}) collective-permute-start(s32[2,2048]{1,0:T(2,128)} %refs_0_.1), channel_id=1, source_target_pairs={{0,24},{8,0},{16,8},{24,16},{1,25},{9,1},{17,9},{25,17},{2,26},{10... | collective-permute-start | bytes 49160 | tf_op jit(solution)/shard_map/ppermute | solution.py:20
  8.6 8.5 %collective-permute-start.3 = (f32[512]{0:T(512)}, f32[512]{0:T(512)S(1)}, u32[]{:S(2)}, u32[]{:S(2)}) collective-permute-start(f32[512]{0:T(512)} %param.9), channel_id=1, source_target_pairs={{4,0},{8,4},{12,8},{16,12},{20,16},{24,20},{28,24},{0,28},{5,1},{9... | collective-permute-start | bytes 6152 | tf_op jit(solution)/shard_map/ppermute | solution.py:29
  17.1 3.7 %collective-permute-start.4 = (f32[1024]{0:T(1024)S(1)}, f32[1024]{0:T(1024)S(1)}, u32[]{:S(2)}, u32[]{:S(2)}) collective-permute-start(f32[1024]{0:T(1024)S(1)} %pad_maximum_fusion.2), channel_id=1, source_target_pairs={{8,0},{12,4},{16,8},{20,12},{24,16},{28,20},{0,24},{4,28},{9,1},{1... | collective-permute-start | bytes 12296 | tf_op jit(solution)/shard_map/ppermute | solution.py:29
  20.8 4.5 %collective-permute-start.5 = (f32[2048]{0:T(1024)S(1)}, f32[2048]{0:T(1024)S(1)}, u32[]{:S(2)}, u32[]{:S(2)}) collective-permute-start(f32[2048]{0:T(1024)S(1)} %pad_maximum_fusion), channel_id=1, source_target_pairs={{16,0},{20,4},{24,8},{28,12},{0,16},{4,20},{8,24},{12,28},{17,1},{... | collective-permute-start | bytes 24584 | tf_op jit(solution)/shard_map/ppermute | solution.py:29
  26.2 0.6 copy-start.1
  26.2 0.6 copy-start.2
  26.2 0.6 copy-start.3

commit v2 on v1

v2 whole, which is shorter than its diff:
```python
import functools
import math

import jax
import jax.numpy as jnp
from jax import lax
from jax.experimental import pallas as pl
from jax.experimental.pallas import tpu as pltpu
from jax.sharding import PartitionSpec as P

B = 256

phase_count = 4096
SINE = (6.2831640442776635, -41.337142367123384, 81.34076873476997, -70.99343163979194)
LEAD = SINE[3]
POLY = tuple(c / LEAD for c in SINE[:3])
VMEM_LIMIT = 58 * 1024 * 1024


def rotated(x, axis):
    count = lax.axis_size(axis)
    shifts = [[(i, (i + k) % count) for i in range(count)] for k in range(1, count)]
    return [x] + [lax.ppermute(x, axis, pairs) for pairs in shifts]


def gathered_doubling(x, axes):
    count = lax.axis_size(axes)
    held, have = x[None], 1
    while have < count:
        take = min(have, count - have)
        pairs = [((i + have) % count, i) for i in range(count)]
        held = jnp.concatenate([held, lax.ppermute(held[:take], axes, pairs)])
        have += take
    return held


def split3(x):
    high = x.astype(jnp.bfloat16)
    rest = x - high.astype(jnp.float32)
    mid = rest.astype(jnp.bfloat16)
    return high, mid, (rest - mid.astype(jnp.float32)).astype(jnp.bfloat16)


def dot_f32(a, b, b_dim):
    ah, am, al = split3(a)
    bh, bm, bl = split3(b)
    return lax.dot_general(
        jnp.concatenate([ah, ah, am, ah, al, am], axis=1),
        jnp.concatenate([bh, bm, bh, bl, bh, bm], axis=b_dim),
        (((1,), (b_dim,)), ((), ())),
        preferred_element_type=jnp.float32,
    )


def factor_panel(t, size, group):
    row = lax.broadcasted_iota(jnp.int32, t.shape, 0)
    for j in range(0, size, group):
        span = range(group)
        cols = [jnp.broadcast_to(t[:, j + k : j + k + 1], t.shape) for k in span]
        rows = [t[j + k : j + k + 1, :] for k in span]
        pivot = [[cols[l][j + k : j + k + 1, :] for l in span] for k in span]
        done = []
        for k in span:
            root = lax.rsqrt(pivot[k][k])
            inverse = root * root
            weight = rows[k] * inverse
            for l in range(k + 1, group):
                lower = pivot[l][k]
                rows[l] = rows[l] - lower * weight
                cols[l] = cols[l] - cols[k] * (pivot[k][l] * inverse)
                for q in range(k + 1, group):
                    pivot[l][q] = pivot[l][q] - lower * (pivot[k][q] * inverse)
            t = t - jnp.where(row >= j + group, cols[k], 0.0) * weight
            done.append(rows[k] * root)
        for k in span:
            t = jnp.where(row == j + k, done[k], t)
    return t


def invert_factor(m_ref, size, group):
    n = m_ref.shape[0]

    @pl.loop(0, n // size)
    def _(k):
        here = pl.ds(pl.multiple_of(k * size, size), size)
        panel = m_ref[here, :]
        lane = lax.broadcasted_iota(jnp.int32, (size, 2 * size), 1)
        row = lax.broadcasted_iota(jnp.int32, (size, 2 * size), 0)
        eye = jnp.where(lane == row, 1.0, 0.0)
        t = jnp.where(
            lane < size, panel[:, : 2 * size], jnp.where(lane - size == row, 1.0, 0.0)
        )
        t = factor_panel(t, size, group)
        inverse = pltpu.roll(t, size, 1)[:, :size]
        first = jnp.where(lane < size, eye, panel[:, : 2 * size])
        done = dot_f32(inverse, jnp.concatenate([first, panel[:, 2 * size :]], axis=1), 0)
        full = m_ref[...]
        below = lax.broadcasted_iota(jnp.int32, (n, size), 0) >= (k + 1) * size
        low = jnp.where(below, dot_f32(full[:, :size], inverse, 1), 0.0)
        kept = jnp.where(lax.broadcasted_iota(jnp.int32, (n, n), 1) < size, 0.0, full)
        m_ref[...] = pltpu.roll(kept - dot_f32(low, done, 0), n - size, 1)
        m_ref[here, :] = pltpu.roll(done, n - size, 1)


def fill_phases(mine, steps_refs, sums_ref, pt_ref):
    here = steps_refs[0].shape[1]
    blocks = here // 128
    count = len(steps_refs)
    for k, ref in enumerate(steps_refs):
        group = lax.rem(mine - k + count, count)
        for b in range(blocks):
            row = pl.multiple_of((group * blocks + b) * 2, 2)
            sums_ref[pl.ds(row, 2), :] = ref[:, b * 128 : (b + 1) * 128].astype(jnp.float32)
    total = sums_ref.shape[0]
    terms = sums_ref[...].astype(jnp.bfloat16)
    i = lax.broadcasted_iota(jnp.int32, (128, 128), 0)
    j = lax.broadcasted_iota(jnp.int32, (128, 128), 1)
    inside = jnp.dot(
        terms, jnp.where(i <= j, 1.0, 0.0).astype(jnp.bfloat16), preferred_element_type=jnp.float32
    )
    ends = jnp.dot(terms, jnp.ones((128, 128), jnp.bfloat16), preferred_element_type=jnp.float32)
    ends = ends.astype(jnp.int32)
    i = lax.broadcasted_iota(jnp.int32, (total, total), 0)
    j = lax.broadcasted_iota(jnp.int32, (total, total), 1)
    earlier = jnp.where((j < i) & ((i - j) % 2 == 0), 1.0, 0.0).astype(jnp.bfloat16)

    def before(x):
        return jnp.dot(
            earlier, x.astype(jnp.float32).astype(jnp.bfloat16), preferred_element_type=jnp.float32
        ).astype(jnp.int32)

    phase = inside.astype(jnp.int32) + before(ends & 127) + before(ends >> 7) * 128
    turn = (phase & (phase_count - 1)).astype(jnp.float32) * (1.0 / phase_count)
    pt_ref[...] = jnp.zeros_like(pt_ref)
    for b in range(total // 2):
        pt_ref[0:2, b * 128 : (b + 1) * 128] = turn[2 * b : 2 * b + 2, :]


def fill_toeplitz(taps_ref, wt_ref):
    count = taps_ref.shape[1]
    taps = taps_ref[...]
    none = jnp.zeros_like(taps)
    for half, row in enumerate(([none, taps], [taps, none])):
        spread = jnp.broadcast_to(jnp.concatenate(row, axis=1), (count, 2 * count))
        spread = pltpu.roll(spread, 0, 1, stride=1, stride_axis=0)
        wt_ref[half * count : (half + 1) * count, :] = spread[:, :count].astype(jnp.bfloat16)


def parameter_table(harmonic, col_scale):
    rows = [harmonic >> 6, harmonic & 63]
    rows = [x.astype(jnp.float32) for x in rows] + [col_scale * (math.sqrt(2.0) * LEAD)]
    return jnp.concatenate(rows + [jnp.zeros((125, harmonic.shape[1]), jnp.float32)]).T


def fill_design(h_ref, pt_ref, d_ref, start, stop, lane, tile):
    here = slice(start, stop)
    p0 = pt_ref[0:1, pl.ds(tile, 256)]
    p1 = pt_ref[1:2, pl.ds(tile, 256)]
    turns = h_ref[here, 0:1] * p0 + h_ref[here, 1:2] * p1 - 0.125
    s = 0.25 - jnp.abs(turns - jnp.round(turns))
    z = s * s
    poly = ((z + POLY[2]) * z + POLY[1]) * z + POLY[0]
    d_ref[here, lane : lane + 256] = (poly * (s * h_ref[here, 2:3])).astype(jnp.bfloat16)


def fill_filtered(d_ref, wt_ref, f_ref, start, stop, block):
    count = wt_ref.shape[1]
    f_ref[start:stop, block * count : (block + 1) * count] = jnp.dot(
        d_ref[start:stop, block * count : (block + 2) * count],
        wt_ref[...],
        preferred_element_type=jnp.float32,
    ).astype(jnp.bfloat16)


def lead_kernel(n_steps, *refs):
    steps_refs = refs[:n_steps]
    harmonic_ref, scale_ref, taps_ref = refs[n_steps : n_steps + 3]
    pt_ref, wt_ref, lead_ref, block_ref = refs[n_steps + 3 : n_steps + 7]
    sums_ref, h_ref, d_ref, f_ref = refs[n_steps + 7 :]
    lead, epochs = lead_ref.shape
    count = wt_ref.shape[1]
    tile = f_ref.shape[1]
    fill_phases(lax.axis_index("epoch"), steps_refs, sums_ref, pt_ref)
    fill_toeplitz(taps_ref, wt_ref)
    h_ref[...] = parameter_table(harmonic_ref[:, :lead], scale_ref[:, :lead])
    d_ref[:, :count] = jnp.zeros((lead, count), jnp.bfloat16)
    block_ref[...] = jnp.zeros_like(block_ref)

    def design(start, row):
        def step():
            for lane in range(0, tile, 256):
                fill_design(h_ref, pt_ref, d_ref, row, row + 16, count + lane, start + lane)
        return step

    for row in range(0, lead, 16):
        design(0, row)()

    @pl.loop(0, epochs // tile)
    def _(step):
        begin = pl.multiple_of(step * tile, tile)
        for b in range(tile // count):
            fill_filtered(d_ref, wt_ref, f_ref, 0, lead, b)
        lead_ref[:, pl.ds(begin, tile)] = f_ref[...]
        d_ref[:, :count] = d_ref[:, tile:]
        following = pl.multiple_of(lax.rem(begin + tile, epochs), tile)
        for row in range(0, lead, 16):
            design(following, row)()
        block_ref[...] += lax.dot_general(
            f_ref[...], f_ref[...], (((1,), (1,)), ((), ())), preferred_element_type=jnp.float32
        )


def main_kernel(shape, *refs):
    rows, lead, cols, n_row = shape
    harmonic_ref, scale_ref, ridge_ref, held_ref, pt_ref, wt_ref, lead_ref, block_ref = refs[:8]
    panel_ref, schur_ref, h_ref, r_ref, d_ref, fa_ref, fb_ref, acc_ref, m_ref = refs[8:]
    width, tile = fa_ref.shape
    count = wt_ref.shape[1]
    step = pl.program_id(0)
    epochs = pt_ref.shape[1]
    mine = lax.axis_index("epoch") * n_row + lax.axis_index("prow")
    first_row = pl.multiple_of(mine * rows, rows)
    first_col = pl.multiple_of(lax.axis_index("pcol") * cols, cols)
    segments = [(0, rows), (rows + lead, width)]

    def design(start, row):
        def run():
            d_ref[row : row + 16, :count] = d_ref[row : row + 16, tile:]
            for lane in range(0, tile, 256):
                fill_design(h_ref, pt_ref, d_ref, row, row + 16, count + lane, start + lane)
        return run

    def filtered(f_ref, begin, end, block):
        return lambda: fill_filtered(d_ref, wt_ref, f_ref, begin, end, block)

    def product(f_ref, begin, end, depth):
        def run():
            acc_ref[:depth, begin:end] += lax.dot_general(
                f_ref[:depth, :],
                f_ref[rows + begin : rows + end, :],
                (((1,), (1,)), ((), ())),
                preferred_element_type=jnp.float32,
            )
        return run

    def products(f_ref):
        pieces = [(0, lead, rows)]
        pieces += [(c, min(c + 256, lead + cols), rows + lead) for c in range(lead, lead + cols, 256)]
        return [product(f_ref, *piece) for piece in pieces]

    @pl.when(step == 0)
    def _():
        table = parameter_table(harmonic_ref[...], scale_ref[...])
        r_ref[...] = table
        h_ref[:rows, :] = r_ref[pl.ds(first_row, rows), :]
        h_ref[rows + lead :, :] = r_ref[pl.ds(first_col, cols), :]
        fb_ref[...] = jnp.zeros_like(fb_ref)
        acc_ref[...] = jnp.zeros_like(acc_ref)
        d_ref[...] = jnp.zeros_like(d_ref)
        for begin, end in segments:
            for row in range(begin, end, 16):
                design(0, row)()

    def phase(f_ref, before_ref, tile_index):
        begin = pl.multiple_of(tile_index * tile, tile)
        following = pl.multiple_of(lax.rem(begin + tile, epochs), tile)
        f_ref[rows : rows + lead, :] = lead_ref[:, pl.ds(begin, tile)]
        chunk = 256
        sets = []
        for start, stop in segments:
            for at in range(start, stop, chunk):
                sets.append((at, min(at + chunk, stop)))
        later = products(before_ref)
        for k, (at, end) in enumerate(sets):
            for b in range(tile // count):
                filtered(f_ref, at, end, b)()
            for n in range(k * len(later) // len(sets), (k + 1) * len(later) // len(sets)):
                later[n]()
            for row in range(at, end, 16):
                design(following, row)()

    phase(fa_ref, fb_ref, 2 * step)
    phase(fb_ref, fa_ref, 2 * step + 1)

    @pl.when(step == pl.num_programs(0) - 1)
    def _():
        for run in products(fb_ref):
            run()
        blocks = held_ref.shape[0]
        mid = -(-rows // 128) * 128
        spare = jnp.zeros((1, mid - rows), jnp.float32) if mid > rows else None
        own = ridge_ref[...] if spare is None else jnp.concatenate([ridge_ref[...], spare], axis=1)
        own = jnp.concatenate([own, jnp.zeros((127, mid), jnp.float32)]).T[:rows, :1]
        first = []
        for q in range(-(-lead // rows)):
            first.append(held_ref[pl.ds(lax.rem(q - mine + blocks, blocks), 1), :])
        first = jnp.concatenate(first, axis=1)[:, :lead]
        first = jnp.concatenate([first, jnp.zeros((127, lead), jnp.float32)]).T[:, :1]
        scale = 1.0 / epochs
        i = lax.broadcasted_iota(jnp.int32, (rows, lead + cols), 0) + first_row
        j = lax.broadcasted_iota(jnp.int32, (rows, lead + cols), 1)
        j = jnp.where(j < lead, j, j - lead + first_col)
        acc_ref[:rows, :] = acc_ref[:rows, :] * scale + jnp.where(i == j, own, 0.0)
        i = lax.broadcasted_iota(jnp.int32, (lead, cols), 0)
        j = lax.broadcasted_iota(jnp.int32, (lead, cols), 1) + first_col
        acc_ref[rows:, lead:] = acc_ref[rows:, lead:] * scale + jnp.where(i == j, first, 0.0)
        i = lax.broadcasted_iota(jnp.int32, (lead, lead), 0)
        j = lax.broadcasted_iota(jnp.int32, (lead, lead), 1)
        m_ref[...] = block_ref[...] * scale + jnp.where(i == j, first, 0.0)
        invert_factor(m_ref, 64, 8)
        inverse = jnp.where(i >= j, m_ref[...], 0.0)
        highest = functools.partial(
            lax.dot_general, precision=lax.Precision.HIGHEST, preferred_element_type=jnp.float32
        )
        panel_ref[...] = highest(acc_ref[:rows, :lead], inverse, (((1,), (1,)), ((), ())))
        for c in range(0, cols, 256):
            solved = highest(inverse, acc_ref[rows:, lead + c : lead + c + 256], (((1,), (0,)), ((), ())))
            schur_ref[:, c : c + 256] = acc_ref[:rows, lead + c : lead + c + 256] - highest(
                panel_ref[...], solved, (((1,), (0,)), ((), ()))
            )


def on_device(steps, harmonic, col_scale, taps, ridge):
    params = harmonic.shape[0]
    n_epoch = lax.axis_size("epoch")
    n_row = lax.axis_size("prow")
    n_col = lax.axis_size("pcol")
    rows = params // (n_epoch * n_row)
    cols = params // n_col
    width = rows + B + cols
    epochs = steps.shape[1] * n_epoch
    count = taps.shape[0]
    tile = 512
    steps_parts = rotated(steps, "epoch")
    held = gathered_doubling(ridge, ("epoch", "prow"))
    row_of = lambda x: x.reshape(1, -1)
    in_vmem = pl.BlockSpec(memory_space=pltpu.VMEM)
    f32 = lambda *shape: jax.ShapeDtypeStruct(shape, jnp.float32)
    bf16 = lambda *shape: jax.ShapeDtypeStruct(shape, jnp.bfloat16)
    params_row, scales_row = row_of(harmonic), row_of(col_scale)
    shared = pl.pallas_call(
        functools.partial(lead_kernel, len(steps_parts)),
        out_shape=(f32(8, epochs), bf16(2 * count, count), bf16(B, epochs), f32(B, B)),
        in_specs=[in_vmem] * (len(steps_parts) + 3),
        out_specs=(in_vmem,) * 4,
        scratch_shapes=[
            pltpu.VMEM((2 * epochs // 128, 128), jnp.float32),
            pltpu.VMEM((B, 128), jnp.float32),
            pltpu.VMEM((B, count + 1024), jnp.bfloat16),
            pltpu.VMEM((B, 1024), jnp.bfloat16),
        ],
        compiler_params=pltpu.CompilerParams(vmem_limit_bytes=VMEM_LIMIT),
    )(*steps_parts, params_row, scales_row, row_of(taps))
    operands = (params_row, scales_row, row_of(ridge), held, *shared)
    return pl.pallas_call(
        functools.partial(main_kernel, (rows, B, cols, n_row)),
        grid=(epochs // (2 * tile),),
        out_shape=(f32(rows, B), f32(rows, cols)),
        in_specs=[in_vmem] * len(operands),
        out_specs=(in_vmem, in_vmem),
        scratch_shapes=[
            pltpu.VMEM((width, 128), jnp.float32),
            pltpu.VMEM((params, 128), jnp.float32),
            pltpu.VMEM((width, count + tile), jnp.bfloat16),
            pltpu.VMEM((width, tile), jnp.bfloat16),
            pltpu.VMEM((width, tile), jnp.bfloat16),
            pltpu.VMEM((rows + B, B + cols), jnp.float32),
            pltpu.VMEM((B, B), jnp.float32),
        ],
        compiler_params=pltpu.CompilerParams(vmem_limit_bytes=VMEM_LIMIT),
    )(*operands)


def solution(mesh):
    in_specs = (P(None, "epoch"), P(), P(), P(), P(("epoch", "prow")))
    out_specs = (P(("epoch", "prow"), None), P(("epoch", "prow"), "pcol"))
    return jax.shard_map(
        on_device, mesh=mesh, in_specs=in_specs, out_specs=out_specs, check_vma=False
    )
```

time: 112 us -> 91.3 us (0.82)
  Pallas kernels: 84.5 us -> 67.7 us
  local copies, waits for them, and re-layouts: 8.83 us -> 0.6 us
  starting transfers between devices: 10.8 us -> 14.2 us
  other arithmetic: 0.18 us -> 2.68 us
  waiting for transfers between devices: 6.25 us -> 4.5 us
    pallas_call x1 -> x2, Pallas kernels: 84.5 us -> 67.7 us  [the longest x1 57.5 us: on_device(): pl.pallas_call(functools.partial(main_kernel, (rows, B, cols, n_row)), gr...]
    ppermute x3, starting transfers between devices: 2.89 us -> 7.78 us  [gathered_doubling(): held = jnp.concatenate([held, lax.ppermute(held[:take], axes, pairs)])]
    dynamic_slice x4 -> x0, local copies, waits for them, and re-layouts: 2.89 us -> none  [the longest x2 1.52 us: own(): lax.dynamic_slice_in_dim(x, first_row, rows)]
    concatenate x3, other arithmetic: 0.02 us -> 2.68 us  [gathered_doubling(): held = jnp.concatenate([held, lax.ppermute(held[:take], axes, pairs)])]
    ppermute x3, waiting for transfers between devices: 6.24 us -> 3.78 us  [gathered_doubling(): held = jnp.concatenate([held, lax.ppermute(held[:take], axes, pairs)])]
    ppermute x3, starting transfers between devices: 7.93 us -> 6.41 us  [rotated(): return [x] + [lax.ppermute(x, axis, pairs) for pairs in shifts]]
    slice x4 -> x0, local copies, waits for them, and re-layouts: 1.48 us -> none  [the longest x2 1.37 us: own(): x[:B]]
    another operation x6 -> x0, local copies, waits for them, and re-layouts: 1.36 us -> none  [the longest x4 0.72 us: on_device(): jnp.stack([orders, degrees, orders, degrees, ones, own(col_scale) * math....]
  transfers between devices with their start and end apart: 6 -> 6, of which waited for: 2 -> 3; matrix products, arithmetic and copies ran while one was open for 8% -> 1% of each run, Pallas kernels for 0% -> 0%
where the time goes in v2:
time: 91.3 us; the launch traced here: 90.3 us
  Pallas kernels  67.7 us (74%)
  starting transfers between devices  14.2 us (16%)
  waiting for transfers between devices  4.5 us (5%)
  other arithmetic  2.68 us (3%)
    pallas_call x1, Pallas kernels, on_device(): pl.pallas_call(functools.partial(main_kernel, (rows, B, cols, n_row)), gr...  57.5 us
    pallas_call x1, Pallas kernels, on_device(): pl.pallas_call(functools.partial(lead_kernel, len(steps_parts)), out_shap...  10.2 us
    ppermute x3, starting transfers between devices, gathered_doubling(): held = jnp.concatenate([held, lax.ppermute(held[:take], axes, pairs)])  7.78 us
    ppermute x3, starting transfers between devices, rotated(): return [x] + [lax.ppermute(x, axis, pairs) for pairs in shifts]  6.41 us
    ppermute x3, waiting for transfers between devices, gathered_doubling(): held = jnp.concatenate([held, lax.ppermute(held[:take], axes, pairs)])  3.78 us
    concatenate x3, other arithmetic, gathered_doubling(): held = jnp.concatenate([held, lax.ppermute(held[:take], axes, pairs)])  2.68 us
  transfers between devices with their start and end apart: 6, of which 3 were waited for; matrix products, arithmetic and copies ran while one was open for 1% of the time, Pallas kernels for 0%

profile of v2, /device:TPU:0, one launch (start us, length us, event | category | flops | bytes accessed | tf_op | source)
XLA Modules:
  0.0 90.3 jit_solution(9635114008923974918)
XLA Ops:
  0.6 6.0 %collective-permute-start = (f32[1,512]{1,0:T(1,128)}, f32[1,512]{1,0:T(1,128)S(1)}, u32[]{:S(2)}, u32[]{:S(2)}) collective-permute-start(f32[1,512]{1,0:T(1,128)} %bitcast.8), channel_id=1, source_target_pairs={{4,0},{8,4},{12,8},{16,12},{20,16},{24,20},{28,24},{0,28},{5,1},{9... | collective-permute-start | bytes 6152 | tf_op jit(solution)/shard_map/ppermute | solution.py:32
  6.7 1.5 %collective-permute-done = f32[1,512]{1,0:T(1,128)S(1)} collective-permute-done((f32[1,512]{1,0:T(1,128)}, f32[1,512]{1,0:T(1,128)S(1)}, u32[]{:S(2)}, u32[]{:S(2)}) %collective-permute-start) | collective-permute-done | bytes 2080 | tf_op jit(solution)/shard_map/ppermute | solution.py:32
  8.2 0.7 pad_maximum_fusion.2
  8.9 1.3 %collective-permute-start.1 = (f32[2,512]{1,0:T(2,128)S(1)}, f32[2,512]{1,0:T(2,128)S(1)}, u32[]{:S(2)}, u32[]{:S(2)}) collective-permute-start(f32[2,512]{1,0:T(2,128)S(1)} %pad_maximum_fusion.2), channel_id=1, source_target_pairs={{8,0},{12,4},{16,8},{20,12},{24,16},{28,20},{0,24},{4,28},{9,1},{1... | collective-permute-start | bytes 12296 | tf_op jit(solution)/shard_map/ppermute | solution.py:32
  10.2 2.3 %collective-permute-done.1 = f32[2,512]{1,0:T(2,128)S(1)} collective-permute-done((f32[2,512]{1,0:T(2,128)S(1)}, f32[2,512]{1,0:T(2,128)S(1)}, u32[]{:S(2)}, u32[]{:S(2)}) %collective-permute-start.1) | collective-permute-done | bytes 4128 | tf_op jit(solution)/shard_map/ppermute | solution.py:32
  12.5 0.7 pad_maximum_fusion.1
  13.2 0.4 collective-permute-start.2
  13.6 2.6 %collective-permute-start.4 = (s32[2,2048]{1,0:T(2,128)}, s32[2,2048]{1,0:T(2,128)S(1)}, u32[]{:S(2)}, u32[]{:S(2)}) collective-permute-start(s32[2,2048]{1,0:T(2,128)} %refs_0_.1), channel_id=1, source_target_pairs={{0,16},{8,24},{16,0},{24,8},{1,17},{9,25},{17,1},{25,9},{2,18},{10... | collective-permute-start | bytes 49160 | tf_op jit(solution)/shard_map/ppermute | solution.py:23
  16.2 0.9 collective-permute-start.3
  17.0 3.0 %collective-permute-start.5 = (s32[2,2048]{1,0:T(2,128)}, s32[2,2048]{1,0:T(2,128)S(1)}, u32[]{:S(2)}, u32[]{:S(2)}) collective-permute-start(s32[2,2048]{1,0:T(2,128)} %refs_0_.1), channel_id=1, source_target_pairs={{0,24},{8,0},{16,8},{24,16},{1,25},{9,1},{17,9},{25,17},{2,26},{10... | collective-permute-start | bytes 49160 | tf_op jit(solution)/shard_map/ppermute | solution.py:23
  20.0 0.0 collective-permute-done.2
  20.0 1.3 %pad_maximum_fusion.refs_3_ = f32[8,512]{1,0:T(8,128)} fusion(f32[4,512]{1,0:T(4,128)S(1)} %collective-permute-done.2, f32[2,512]{1,0:T(2,128)S(1)} %collective-permute-done.1, f32[1,512]{1,0:T(1,128)S(1)} %collective-permute-done, f32[1,512]{1,0:T(1,128)} %bitcast.11), kind=kLoop, calls=%fused_computation | loop fusion | flops 12288 | bytes 32768 | tf_op jit(solution)/shard_map/concatenate | solution.py:32
  21.3 0.0 collective-permute-done.4.refs_2_
  21.3 0.0 copy-start
  21.3 0.7 collective-permute-done.3.refs_1_
  22.0 0.0 copy-start.1
  22.0 0.0 collective-permute-done.5.refs_3_
  22.0 0.0 copy-start.2
  22.0 0.0 copy-done
  22.0 0.6 copy-done.1
  22.6 0.0 copy-done.2
  22.6 10.2 %shard_map.68 = (f32[8,8192]{1,0:T(8,128)}, bf16[512,256]{1,0:T(8,128)(2,1)}, bf16[256,8192]{1,0:T(8,128)(2,1)}, f32[256,256]{1,0:T(8,128)}) custom-call(s32[2,2048]{1,0:T(2,128)} %refs_0_.1, s32[2,2048]{1,0:T(2,128)} %copy-done.1, s32[2,2048]{1,0:T(2,128)} %copy-done, s32[2,2048]{1,0:T(2,128)} %copy-done.2, s32[1,4096]{1,0:T(1,128)} %bitcast.4, ...), custom_call_target="tpu_custom_call" | custom-call | tf_op jit(solution)/shard_map/pallas_call | solution.py:341
  32.8 57.5 %shard_map.69 = (f32[512,256]{1,0:T(8,128)}, f32[512,1024]{1,0:T(8,128)}) custom-call(s32[1,4096]{1,0:T(1,128)} %bitcast.5, f32[1,4096]{1,0:T(1,128)} %bitcast.7, f32[1,512]{1,0:T(1,128)} %bitcast.12, f32[8,512]{1,0:T(8,128)} %pad_maximum_fusion.refs_3_, f32[8,8192]{1,0:T(8,128)} %get-tuple-element.6.refs_4_, bf16[512,256]{1,0:T(8,128)(2,1)} %get-tuple-element.7.refs_5_, ...), custom_call_target="tpu_custom_call" | custom-call | tf_op jit(solution)/shard_map/pallas_call | solution.py:355
Async XLA Ops:
  0.6 7.5 %collective-permute-start = (f32[1,512]{1,0:T(1,128)}, f32[1,512]{1,0:T(1,128)S(1)}, u32[]{:S(2)}, u32[]{:S(2)}) collective-permute-start(f32[1,512]{1,0:T(1,128)} %bitcast.8), channel_id=1, source_target_pairs={{4,0},{8,4},{12,8},{16,12},{20,16},{24,20},{28,24},{0,28},{5,1},{9... | collective-permute-start | bytes 6152 | tf_op jit(solution)/shard_map/ppermute | solution.py:32
  8.9 3.6 %collective-permute-start.1 = (f32[2,512]{1,0:T(2,128)S(1)}, f32[2,512]{1,0:T(2,128)S(1)}, u32[]{:S(2)}, u32[]{:S(2)}) collective-permute-start(f32[2,512]{1,0:T(2,128)S(1)} %pad_maximum_fusion.2), channel_id=1, source_target_pairs={{8,0},{12,4},{16,8},{20,12},{24,16},{28,20},{0,24},{4,28},{9,1},{1... | collective-permute-start | bytes 12296 | tf_op jit(solution)/shard_map/ppermute | solution.py:32
  13.2 6.8 %collective-permute-start.2 = (f32[4,512]{1,0:T(4,128)S(1)}, f32[4,512]{1,0:T(4,128)S(1)}, u32[]{:S(2)}, u32[]{:S(2)}) collective-permute-start(f32[4,512]{1,0:T(4,128)S(1)} %pad_maximum_fusion.1), channel_id=1, source_target_pairs={{16,0},{20,4},{24,8},{28,12},{0,16},{4,20},{8,24},{12,28},{17,1},{... | collective-permute-start | bytes 24584 | tf_op jit(solution)/shard_map/ppermute | solution.py:32
  13.6 7.7 %collective-permute-start.4 = (s32[2,2048]{1,0:T(2,128)}, s32[2,2048]{1,0:T(2,128)S(1)}, u32[]{:S(2)}, u32[]{:S(2)}) collective-permute-start(s32[2,2048]{1,0:T(2,128)} %refs_0_.1), channel_id=1, source_target_pairs={{0,16},{8,24},{16,0},{24,8},{1,17},{9,25},{17,1},{25,9},{2,18},{10... | collective-permute-start | bytes 49160 | tf_op jit(solution)/shard_map/ppermute | solution.py:23
  16.2 5.8 %collective-permute-start.3 = (s32[2,2048]{1,0:T(2,128)}, s32[2,2048]{1,0:T(2,128)S(1)}, u32[]{:S(2)}, u32[]{:S(2)}) collective-permute-start(s32[2,2048]{1,0:T(2,128)} %refs_0_.1), channel_id=1, source_target_pairs={{0,8},{8,16},{16,24},{24,0},{1,9},{9,17},{17,25},{25,1},{2,10},{10... | collective-permute-start | bytes 49160 | tf_op jit(solution)/shard_map/ppermute | solution.py:23
  17.0 5.0 %collective-permute-start.5 = (s32[2,2048]{1,0:T(2,128)}, s32[2,2048]{1,0:T(2,128)S(1)}, u32[]{:S(2)}, u32[]{:S(2)}) collective-permute-start(s32[2,2048]{1,0:T(2,128)} %refs_0_.1), channel_id=1, source_target_pairs={{0,24},{8,0},{16,8},{24,16},{1,25},{9,1},{17,9},{25,17},{2,26},{10... | collective-permute-start | bytes 49160 | tf_op jit(solution)/shard_map/ppermute | solution.py:23
  21.3 0.7 copy-start
  22.0 0.6 copy-start.1
  22.0 0.6 copy-start.2

commit v3 on v2

--- a/solution.py
+++ b/solution.py
@@ -15,23 +15,13 @@
 LEAD = SINE[3]
 POLY = tuple(c / LEAD for c in SINE[:3])
 VMEM_LIMIT = 58 * 1024 * 1024
+FACTOR_BLOCK, FACTOR_GROUP, FACTOR_PARTS = 32, 8, 4
 
 
 def rotated(x, axis):
     count = lax.axis_size(axis)
     shifts = [[(i, (i + k) % count) for i in range(count)] for k in range(1, count)]
     return [x] + [lax.ppermute(x, axis, pairs) for pairs in shifts]
-
-
-def gathered_doubling(x, axes):
-    count = lax.axis_size(axes)
-    held, have = x[None], 1
-    while have < count:
-        take = min(have, count - have)
-        pairs = [((i + have) % count, i) for i in range(count)]
-        held = jnp.concatenate([held, lax.ppermute(held[:take], axes, pairs)])
-        have += take
-    return held
 
 
 def split3(x):
@@ -52,9 +42,9 @@
     )
 
 
-def factor_panel(t, size, group):
+def factor_panel(t, first, last, group):
     row = lax.broadcasted_iota(jnp.int32, t.shape, 0)
-    for j in range(0, size, group):
+    for j in range(first, last, group):
         span = range(group)
         cols = [jnp.broadcast_to(t[:, j + k : j + k + 1], t.shape) for k in span]
         rows = [t[j + k : j + k + 1, :] for k in span]
@@ -77,40 +67,57 @@
     return t
 
 
-def invert_factor(m_ref, size, group):
+def factor_steps(m_ref, k, size, group, parts):
     n = m_ref.shape[0]
-
-    @pl.loop(0, n // size)
-    def _(k):
-        here = pl.ds(pl.multiple_of(k * size, size), size)
+    active = k < n // size
+    here = pl.ds(pl.multiple_of(jnp.minimum(k, n // size - 1) * size, size), size)
+    held = {}
+
+    def ids(shape):
+        return [lax.broadcasted_iota(jnp.int32, shape, d) for d in (0, 1)]
+
+    def begin():
+        row, lane = ids((size, 128))
         panel = m_ref[here, :]
-        lane = lax.broadcasted_iota(jnp.int32, (size, 2 * size), 1)
-        row = lax.broadcasted_iota(jnp.int32, (size, 2 * size), 0)
-        eye = jnp.where(lane == row, 1.0, 0.0)
-        t = jnp.where(
-            lane < size, panel[:, : 2 * size], jnp.where(lane - size == row, 1.0, 0.0)
+        held["t"] = jnp.where(
+            lane < size, panel[:, :128], jnp.where(lane - size == row, 1.0, 0.0)
         )
-        t = factor_panel(t, size, group)
-        inverse = pltpu.roll(t, size, 1)[:, :size]
-        first = jnp.where(lane < size, eye, panel[:, : 2 * size])
-        done = dot_f32(inverse, jnp.concatenate([first, panel[:, 2 * size :]], axis=1), 0)
+
+    def eliminate(first, last):
+        def run():
+            held["t"] = factor_panel(held["t"], first, last, group)
+        return run
+
+    def solve():
+        row, lane = ids((size, 128))
+        panel = m_ref[here, :]
+        inverse = pltpu.roll(held["t"], 128 - size, 1)[:, :size]
+        head = jnp.where(lane < size, jnp.where(lane == row, 1.0, 0.0), panel[:, :128])
+        held["done"] = dot_f32(inverse, jnp.concatenate([head, panel[:, 128:]], axis=1), 0)
+        low = dot_f32(m_ref[:, :size], inverse, 1)
+        held["low"] = jnp.where(ids((n, size))[0] >= (k + 1) * size, low, 0.0)
+
+    def update():
         full = m_ref[...]
-        below = lax.broadcasted_iota(jnp.int32, (n, size), 0) >= (k + 1) * size
-        low = jnp.where(below, dot_f32(full[:, :size], inverse, 1), 0.0)
-        kept = jnp.where(lax.broadcasted_iota(jnp.int32, (n, n), 1) < size, 0.0, full)
-        m_ref[...] = pltpu.roll(kept - dot_f32(low, done, 0), n - size, 1)
-        m_ref[here, :] = pltpu.roll(done, n - size, 1)
-
-
-def fill_phases(mine, steps_refs, sums_ref, pt_ref):
-    here = steps_refs[0].shape[1]
-    blocks = here // 128
-    count = len(steps_refs)
-    for k, ref in enumerate(steps_refs):
+        row, lane = ids((n, n))
+        new = jnp.where(lane < size, 0.0, full) - dot_f32(held["low"], held["done"], 0)
+        panel = m_ref[here, :]
+        m_ref[...] = jnp.where(active, pltpu.roll(new, n - size, 1), full)
+        m_ref[here, :] = jnp.where(active, pltpu.roll(held["done"], n - size, 1), panel)
+
+    pieces = [begin]
+    for p in range(parts):
+        pieces.append(eliminate(p * size // parts, (p + 1) * size // parts))
+    return pieces + [solve, update]
+
+
+def fill_phases(mine, parts_refs, sums_ref, pt_ref):
+    count = len(parts_refs)
+    each = sums_ref.shape[0] // count
+    blocks = each // 2
+    for k, ref in enumerate(parts_refs):
         group = lax.rem(mine - k + count, count)
-        for b in range(blocks):
-            row = pl.multiple_of((group * blocks + b) * 2, 2)
-            sums_ref[pl.ds(row, 2), :] = ref[:, b * 128 : (b + 1) * 128].astype(jnp.float32)
+        sums_ref[pl.ds(pl.multiple_of(group * each, each), each), :] = ref[:each, :]
     total = sums_ref.shape[0]
     terms = sums_ref[...].astype(jnp.bfloat16)
     i = lax.broadcasted_iota(jnp.int32, (128, 128), 0)
@@ -122,7 +129,12 @@
     ends = ends.astype(jnp.int32)
     i = lax.broadcasted_iota(jnp.int32, (total, total), 0)
     j = lax.broadcasted_iota(jnp.int32, (total, total), 1)
-    earlier = jnp.where((j < i) & ((i - j) % 2 == 0), 1.0, 0.0).astype(jnp.bfloat16)
+    earlier = jnp.zeros((total, total), jnp.bool_)
+    for track in range(2):
+        mine_i = lax.rem(i, each) // blocks == track
+        mine_j = lax.rem(j, each) // blocks == track
+        earlier = earlier | (mine_i & mine_j & (j < i))
+    earlier = jnp.where(earlier, 1.0, 0.0).astype(jnp.bfloat16)
 
     def before(x):
         return jnp.dot(
@@ -132,8 +144,11 @@
     phase = inside.astype(jnp.int32) + before(ends & 127) + before(ends >> 7) * 128
     turn = (phase & (phase_count - 1)).astype(jnp.float32) * (1.0 / phase_count)
     pt_ref[...] = jnp.zeros_like(pt_ref)
-    for b in range(total // 2):
-        pt_ref[0:2, b * 128 : (b + 1) * 128] = turn[2 * b : 2 * b + 2, :]
+    for r in range(total):
+        group, rest = divmod(r, each)
+        track, b = divmod(rest, blocks)
+        lane = (group * blocks + b) * 128
+        pt_ref[track : track + 1, lane : lane + 128] = turn[r : r + 1, :]
 
 
 def fill_toeplitz(taps_ref, wt_ref):
@@ -172,48 +187,52 @@
     ).astype(jnp.bfloat16)
 
 
-def lead_kernel(n_steps, *refs):
-    steps_refs = refs[:n_steps]
-    harmonic_ref, scale_ref, taps_ref = refs[n_steps : n_steps + 3]
-    pt_ref, wt_ref, lead_ref, block_ref = refs[n_steps + 3 : n_steps + 7]
-    sums_ref, h_ref, d_ref, f_ref = refs[n_steps + 7 :]
-    lead, epochs = lead_ref.shape
+def lead_kernel(n_parts, *refs):
+    parts_refs = refs[:n_parts]
+    harmonic_ref, scale_ref, taps_ref = refs[n_parts : n_parts + 3]
+    pt_ref, wt_ref, lead_ref, block_ref = refs[n_parts + 3 : n_parts + 7]
+    sums_ref, h_ref, d_ref = refs[n_parts + 7 :]
+    lead, tile = lead_ref.shape
+    epochs = pt_ref.shape[1]
     count = wt_ref.shape[1]
-    tile = f_ref.shape[1]
-    fill_phases(lax.axis_index("epoch"), steps_refs, sums_ref, pt_ref)
-    fill_toeplitz(taps_ref, wt_ref)
-    h_ref[...] = parameter_table(harmonic_ref[:, :lead], scale_ref[:, :lead])
-    d_ref[:, :count] = jnp.zeros((lead, count), jnp.bfloat16)
-    block_ref[...] = jnp.zeros_like(block_ref)
-
-    def design(start, row):
-        def step():
-            for lane in range(0, tile, 256):
-                fill_design(h_ref, pt_ref, d_ref, row, row + 16, count + lane, start + lane)
-        return step
-
-    for row in range(0, lead, 16):
-        design(0, row)()
-
-    @pl.loop(0, epochs // tile)
-    def _(step):
-        begin = pl.multiple_of(step * tile, tile)
+    step = pl.program_id(0)
+
+    def design(start, block):
+        for row in range(0, lead, 16):
+            fill_design(
+                h_ref, pt_ref, d_ref, row, row + 16, (block + 1) * count, start + block * count
+            )
+
+    @pl.when(step == 0)
+    def _():
+        fill_phases(lax.axis_index("epoch"), parts_refs, sums_ref, pt_ref)
+        fill_toeplitz(taps_ref, wt_ref)
+        h_ref[...] = parameter_table(harmonic_ref[:, :lead], scale_ref[:, :lead])
+        d_ref[:, :count] = jnp.zeros((lead, count), jnp.bfloat16)
+        block_ref[...] = jnp.zeros_like(block_ref)
         for b in range(tile // count):
-            fill_filtered(d_ref, wt_ref, f_ref, 0, lead, b)
-        lead_ref[:, pl.ds(begin, tile)] = f_ref[...]
-        d_ref[:, :count] = d_ref[:, tile:]
-        following = pl.multiple_of(lax.rem(begin + tile, epochs), tile)
-        for row in range(0, lead, 16):
-            design(following, row)()
-        block_ref[...] += lax.dot_general(
-            f_ref[...], f_ref[...], (((1,), (1,)), ((), ())), preferred_element_type=jnp.float32
-        )
+            design(0, b)
+
+    following = pl.multiple_of(lax.rem((step + 1) * tile, epochs), tile)
+    blocks = tile // count
+    for b in range(blocks):
+        fill_filtered(d_ref, wt_ref, lead_ref, 0, lead, b)
+        if b == min(1, blocks - 1):
+            d_ref[:, :count] = d_ref[:, tile:]
+        if b > 0:
+            design(following, b - 1)
+    design(following, blocks - 1)
+    block_ref[...] += lax.dot_general(
+        lead_ref[...], lead_ref[...], (((1,), (1,)), ((), ())), preferred_element_type=jnp.float32
+    )
 
 
 def main_kernel(shape, *refs):
     rows, lead, cols, n_row = shape
-    harmonic_ref, scale_ref, ridge_ref, held_ref, pt_ref, wt_ref, lead_ref, block_ref = refs[:8]
-    panel_ref, schur_ref, h_ref, r_ref, d_ref, fa_ref, fb_ref, acc_ref, m_ref = refs[8:]
+    harmonic_ref, scale_ref, ridge_ref = refs[:3]
+    held_refs = refs[3 : 3 + n_row]
+    pt_ref, wt_ref, lead_ref, block_ref = refs[3 + n_row : 7 + n_row]
+    panel_ref, schur_ref, h_ref, r_ref, d_ref, fa_ref, fb_ref, acc_ref, m_ref, first_ref = refs[7 + n_row :]
     width, tile = fa_ref.shape
     count = wt_ref.shape[1]
     step = pl.program_id(0)
@@ -257,14 +276,27 @@
         fb_ref[...] = jnp.zeros_like(fb_ref)
         acc_ref[...] = jnp.zeros_like(acc_ref)
         d_ref[...] = jnp.zeros_like(d_ref)
+        n_epoch = held_refs[0].shape[0]
+        first = []
+        for q in range(-(-lead // rows)):
+            for k, ref in enumerate(held_refs):
+                group = lax.rem(lax.axis_index("prow") - k + n_row, n_row)
+                block = lax.rem(lax.axis_index("epoch") - q // n_row + n_epoch, n_epoch)
+                term = jnp.where(group == q % n_row, ref[pl.ds(block, 1), :rows], 0.0)
+                total = term if k == 0 else total + term
+            first.append(total)
+        first = jnp.concatenate(first, axis=1)[:, :lead]
+        first_ref[...] = jnp.concatenate([first, jnp.zeros((127, lead), jnp.float32)]).T
+        i = lax.broadcasted_iota(jnp.int32, (lead, lead), 0)
+        j = lax.broadcasted_iota(jnp.int32, (lead, lead), 1)
+        m_ref[...] = block_ref[...] * (1.0 / epochs) + jnp.where(i == j, first_ref[:, :1], 0.0)
         for begin, end in segments:
             for row in range(begin, end, 16):
                 design(0, row)()
 
-    def phase(f_ref, before_ref, tile_index):
-        begin = pl.multiple_of(tile_index * tile, tile)
-        following = pl.multiple_of(lax.rem(begin + tile, epochs), tile)
-        f_ref[rows : rows + lead, :] = lead_ref[:, pl.ds(begin, tile)]
+    def phase(f_ref, before_ref, half, extra):
+        following = pl.multiple_of(lax.rem((2 * step + half + 1) * tile, epochs), tile)
+        f_ref[rows : rows + lead, :] = lead_ref[:, half * tile : (half + 1) * tile]
         chunk = 256
         sets = []
         for start, stop in segments:
@@ -278,24 +310,23 @@
                 later[n]()
             for row in range(at, end, 16):
                 design(following, row)()
-
-    phase(fa_ref, fb_ref, 2 * step)
-    phase(fb_ref, fa_ref, 2 * step + 1)
+            for n in range(k * len(extra) // len(sets), (k + 1) * len(extra) // len(sets)):
+                extra[n]()
+
+    pieces = factor_steps(m_ref, step, FACTOR_BLOCK, FACTOR_GROUP, FACTOR_PARTS)
+    phase(fa_ref, fb_ref, 0, pieces[: len(pieces) // 2])
+    phase(fb_ref, fa_ref, 1, pieces[len(pieces) // 2 :])
 
     @pl.when(step == pl.num_programs(0) - 1)
     def _():
         for run in products(fb_ref):
             run()
-        blocks = held_ref.shape[0]
         mid = -(-rows // 128) * 128
-        spare = jnp.zeros((1, mid - rows), jnp.float32) if mid > rows else None
-        own = ridge_ref[...] if spare is None else jnp.concatenate([ridge_ref[...], spare], axis=1)
+        own = ridge_ref[...]
+        if mid > rows:
+            own = jnp.concatenate([own, jnp.zeros((1, mid - rows), jnp.float32)], axis=1)
         own = jnp.concatenate([own, jnp.zeros((127, mid), jnp.float32)]).T[:rows, :1]
-        first = []
-        for q in range(-(-lead // rows)):
-            first.append(held_ref[pl.ds(lax.rem(q - mine + blocks, blocks), 1), :])
-        first = jnp.concatenate(first, axis=1)[:, :lead]
-        first = jnp.concatenate([first, jnp.zeros((127, lead), jnp.float32)]).T[:, :1]
+        first = first_ref[:, :1]
         scale = 1.0 / epochs
         i = lax.broadcasted_iota(jnp.int32, (rows, lead + cols), 0) + first_row
         j = lax.broadcasted_iota(jnp.int32, (rows, lead + cols), 1)
@@ -306,8 +337,12 @@
         acc_ref[rows:, lead:] = acc_ref[rows:, lead:] * scale + jnp.where(i == j, first, 0.0)
         i = lax.broadcasted_iota(jnp.int32, (lead, lead), 0)
         j = lax.broadcasted_iota(jnp.int32, (lead, lead), 1)
-        m_ref[...] = block_ref[...] * scale + jnp.where(i == j, first, 0.0)
-        invert_factor(m_ref, 64, 8)
+
+        @pl.loop(epochs // (2 * tile), max(lead // FACTOR_BLOCK, epochs // (2 * tile)))
+        def _(k):
+            for run in factor_steps(m_ref, k, FACTOR_BLOCK, FACTOR_GROUP, FACTOR_PARTS):
+                run()
+
         inverse = jnp.where(i >= j, m_ref[...], 0.0)
         highest = functools.partial(
             lax.dot_general, precision=lax.Precision.HIGHEST, preferred_element_type=jnp.float32
@@ -331,32 +366,43 @@
     epochs = steps.shape[1] * n_epoch
     count = taps.shape[0]
     tile = 512
-    steps_parts = rotated(steps, "epoch")
-    held = gathered_doubling(ridge, ("epoch", "prow"))
+    lead_tile = 1024
+    step_rows = 2 * steps.shape[1] // 128
+    ridge_rows = -(-rows // 128)
+    packed = jnp.concatenate(
+        [
+            steps.astype(jnp.float32).reshape(step_rows, 128),
+            jnp.pad(ridge, (0, ridge_rows * 128 - rows)).reshape(ridge_rows, 128),
+        ]
+    )
+    parts = rotated(packed, "epoch")
+    held = jnp.stack([x[step_rows:].reshape(-1) for x in parts])
+    held = rotated(held, "prow")
     row_of = lambda x: x.reshape(1, -1)
     in_vmem = pl.BlockSpec(memory_space=pltpu.VMEM)
     f32 = lambda *shape: jax.ShapeDtypeStruct(shape, jnp.float32)
     bf16 = lambda *shape: jax.ShapeDtypeStruct(shape, jnp.bfloat16)
     params_row, scales_row = row_of(harmonic), row_of(col_scale)
     shared = pl.pallas_call(
-        functools.partial(lead_kernel, len(steps_parts)),
+        functools.partial(lead_kernel, len(parts)),
+        grid=(epochs // lead_tile,),
         out_shape=(f32(8, epochs), bf16(2 * count, count), bf16(B, epochs), f32(B, B)),
-        in_specs=[in_vmem] * (len(steps_parts) + 3),
-        out_specs=(in_vmem,) * 4,
+        in_specs=[in_vmem] * (len(parts) + 3),
+        out_specs=(in_vmem, in_vmem, pl.BlockSpec((B, lead_tile), lambda i: (0, i)), in_vmem),
         scratch_shapes=[
             pltpu.VMEM((2 * epochs // 128, 128), jnp.float32),
             pltpu.VMEM((B, 128), jnp.float32),
-            pltpu.VMEM((B, count + 1024), jnp.bfloat16),
-            pltpu.VMEM((B, 1024), jnp.bfloat16),
+            pltpu.VMEM((B, count + lead_tile), jnp.bfloat16),
         ],
         compiler_params=pltpu.CompilerParams(vmem_limit_bytes=VMEM_LIMIT),
-    )(*steps_parts, params_row, scales_row, row_of(taps))
-    operands = (params_row, scales_row, row_of(ridge), held, *shared)
+    )(*parts, params_row, scales_row, row_of(taps))
+    operands = (params_row, scales_row, row_of(ridge), *held, *shared)
     return pl.pallas_call(
         functools.partial(main_kernel, (rows, B, cols, n_row)),
         grid=(epochs // (2 * tile),),
         out_shape=(f32(rows, B), f32(rows, cols)),
-        in_specs=[in_vmem] * len(operands),
+        in_specs=[in_vmem] * (len(operands) - 2)
+        + [pl.BlockSpec((B, 2 * tile), lambda i: (0, i)), in_vmem],
         out_specs=(in_vmem, in_vmem),
         scratch_shapes=[
             pltpu.VMEM((width, 128), jnp.float32),
@@ -366,6 +412,7 @@
             pltpu.VMEM((width, tile), jnp.bfloat16),
             pltpu.VMEM((rows + B, B + cols), jnp.float32),
             pltpu.VMEM((B, B), jnp.float32),
+            pltpu.VMEM((B, 128), jnp.float32),
         ],
         compiler_params=pltpu.CompilerParams(vmem_limit_bytes=VMEM_LIMIT),
     )(*operands)

time: 91.3 us -> 82 us (0.90)
  starting transfers between devices: 14.2 us -> 7.62 us
  Pallas kernels: 67.7 us -> 66.1 us
    ppermute x3 -> x0, starting transfers between devices: 7.78 us -> none  [gathered_doubling(): held = jnp.concatenate([held, lax.ppermute(held[:take], axes, pairs)])]
    ppermute x3 -> x4, waiting for transfers between devices: 0.72 us -> 4.56 us  [rotated(): return [x] + [lax.ppermute(x, axis, pairs) for pairs in shifts]]
    ppermute x3 -> x0, waiting for transfers between devices: 3.78 us -> none  [gathered_doubling(): held = jnp.concatenate([held, lax.ppermute(held[:take], axes, pairs)])]
    concatenate x3 -> x1, other arithmetic: 2.68 us -> 0.69 us  [on_device(): jnp.concatenate([steps.astype(jnp.float32).reshape(step_rows, 128), jnp.p...]
    ppermute x3 -> x4, starting transfers between devices: 6.41 us -> 7.62 us  [rotated(): return [x] + [lax.ppermute(x, axis, pairs) for pairs in shifts]]
    pallas_call x1, Pallas kernels: 10.2 us -> 9.18 us  [on_device(): pl.pallas_call(functools.partial(lead_kernel, len(parts)), grid=(epochs /...]
  transfers between devices with their start and end apart: 6 -> 4, of which waited for: 3 -> 3; matrix products, arithmetic and copies ran while one was open for 1% -> 0% of each run, Pallas kernels for 0% -> 11%
where the time goes in v3:
time: 82 us; the launch traced here: 81.7 us
  Pallas kernels  66.1 us (81%)
  starting transfers between devices  7.62 us (9%)
  waiting for transfers between devices  4.56 us (6%)
  other arithmetic  2.12 us (3%)
    pallas_call x1, Pallas kernels, on_device(): pl.pallas_call(functools.partial(main_kernel, (rows, B, cols, n_row)), gr...  56.9 us
    pallas_call x1, Pallas kernels, on_device(): pl.pallas_call(functools.partial(lead_kernel, len(parts)), grid=(epochs /...  9.18 us
    ppermute x4, starting transfers between devices, rotated(): return [x] + [lax.ppermute(x, axis, pairs) for pairs in shifts]  7.62 us
    ppermute x4, waiting for transfers between devices, rotated(): return [x] + [lax.ppermute(x, axis, pairs) for pairs in shifts]  4.56 us
  transfers between devices with their start and end apart: 4, of which 3 were waited for; matrix products, arithmetic and copies ran while one was open for 0% of the time, Pallas kernels for 11%

profile of v3, /device:TPU:0, one launch (start us, length us, event | category | flops | bytes accessed | tf_op | source)
XLA Modules:
  0.0 81.7 jit_solution(2432707700961483510)
XLA Ops:
  0.6 0.7 convert_element_type.3
  1.4 0.7 pad_maximum_fusion.refs_0_
  2.1 0.0 copy-start
  2.1 5.0 %collective-permute-start.2 = (f32[36,128]{1,0:T(8,128)S(1)}, f32[36,128]{1,0:T(8,128)S(1)}, u32[]{:S(2)}, u32[]{:S(2)}) collective-permute-start(f32[36,128]{1,0:T(8,128)S(1)} %pad_maximum_fusion.refs_0_), channel_id=1, source_target_pairs={{0,24},{8,0},{16,8},{24,16},{1,25},{9,1},{17,9},{25,17},{2,26},{10... | collective-permute-start | bytes 55304 | tf_op jit(solution)/shard_map/ppermute | solution.py:24
  7.1 0.0 collective-permute-start.1
  7.1 1.0 %collective-permute-start = (f32[36,128]{1,0:T(8,128)S(1)}, f32[36,128]{1,0:T(8,128)S(1)}, u32[]{:S(2)}, u32[]{:S(2)}) collective-permute-start(f32[36,128]{1,0:T(8,128)S(1)} %pad_maximum_fusion.refs_0_), channel_id=1, source_target_pairs={{0,8},{8,16},{16,24},{24,0},{1,9},{9,17},{17,25},{25,1},{2,10},{10... | collective-permute-start | bytes 55304 | tf_op jit(solution)/shard_map/ppermute | solution.py:24
  8.1 0.5 collective-permute-done.2.refs_3_
  8.6 0.0 copy-start.2
  8.6 3.2 %collective-permute-done.1.refs_2_ = f32[36,128]{1,0:T(8,128)S(1)} collective-permute-done((f32[36,128]{1,0:T(8,128)S(1)}, f32[36,128]{1,0:T(8,128)S(1)}, u32[]{:S(2)}, u32[]{:S(2)}) %collective-permute-start.1) | collective-permute-done | bytes 18464 | tf_op jit(solution)/shard_map/ppermute | solution.py:24
  11.8 0.0 copy-start.3
  11.8 0.9 %collective-permute-done.refs_1_ = f32[36,128]{1,0:T(8,128)S(1)} collective-permute-done((f32[36,128]{1,0:T(8,128)S(1)}, f32[36,128]{1,0:T(8,128)S(1)}, u32[]{:S(2)}, u32[]{:S(2)}) %collective-permute-start) | collective-permute-done | bytes 18464 | tf_op jit(solution)/shard_map/ppermute | solution.py:24
  12.7 0.0 copy-start.4
  12.7 0.7 pad_maximum_fusion.1.refs_3_
  13.4 0.0 copy-start.1
  13.4 1.6 %collective-permute-start.3 = (f32[4,512]{1,0:T(4,128)S(1)}, f32[4,512]{1,0:T(4,128)S(1)}, u32[]{:S(2)}, u32[]{:S(2)}) collective-permute-start(f32[4,512]{1,0:T(4,128)S(1)} %pad_maximum_fusion.1.refs_3_), channel_id=1, source_target_pairs={{0,4},{4,0},{1,5},{5,1},{2,6},{6,2},{3,7},{7,3},{8,12},{12,8},{9,1... | collective-permute-start | bytes 24584 | tf_op jit(solution)/shard_map/ppermute | solution.py:24
  15.0 0.0 copy-done
  15.0 0.0 copy-done.2
  15.0 0.0 copy-done.3
  15.0 0.0 copy-done.4
  15.0 9.2 %shard_map.68 = (f32[8,8192]{1,0:T(8,128)}, bf16[512,256]{1,0:T(8,128)(2,1)}, bf16[256,8192]{1,0:T(8,128)(2,1)}, f32[256,256]{1,0:T(8,128)}) custom-call(f32[36,128]{1,0:T(8,128)} %copy-done, f32[36,128]{1,0:T(8,128)} %copy-done.4, f32[36,128]{1,0:T(8,128)} %copy-done.3, f32[36,128]{1,0:T(8,128)} %copy-done.2, s32[1,4096]{1,0:T(1,128)} %bitcast.8, ...), custom_call_target="tpu_custom_call" | custom-call | tf_op jit(solution)/shard_map/pallas_call | solution.py:386
  24.2 0.0 collective-permute-done.3.refs_4_
  24.2 0.0 copy-start.5
  24.2 0.0 copy-done.1
  24.2 0.6 copy-done.5
  24.8 56.9 %shard_map.69 = (f32[512,256]{1,0:T(8,128)}, f32[512,1024]{1,0:T(8,128)}) custom-call(s32[1,4096]{1,0:T(1,128)} %bitcast.9, f32[1,4096]{1,0:T(1,128)} %bitcast.11, f32[1,512]{1,0:T(1,128)} %bitcast.14, f32[4,512]{1,0:T(4,128)} %copy-done.1, f32[4,512]{1,0:T(4,128)} %copy-done.5, f32[8,8192]{1,0:T(8,128)} %get-tuple-element.6.refs_5_, ...), custom_call_target="tpu_custom_call" | custom-call | tf_op jit(solution)/shard_map/pallas_call | solution.py:400
  (4 shorter events, 0.0 us)
Async XLA Ops:
  2.1 12.9 %copy-start = (f32[36,128]{1,0:T(8,128)}, f32[36,128]{1,0:T(8,128)S(1)}, u32[]{:S(2)}) copy-start(f32[36,128]{1,0:T(8,128)S(1)} %pad_maximum_fusion.refs_0_) | copy-start | bytes 55300
  2.1 6.5 %collective-permute-start.2 = (f32[36,128]{1,0:T(8,128)S(1)}, f32[36,128]{1,0:T(8,128)S(1)}, u32[]{:S(2)}, u32[]{:S(2)}) collective-permute-start(f32[36,128]{1,0:T(8,128)S(1)} %pad_maximum_fusion.refs_0_), channel_id=1, source_target_pairs={{0,24},{8,0},{16,8},{24,16},{1,25},{9,1},{17,9},{25,17},{2,26},{10... | collective-permute-start | bytes 55304 | tf_op jit(solution)/shard_map/ppermute | solution.py:24
  7.1 4.7 %collective-permute-start.1 = (f32[36,128]{1,0:T(8,128)S(1)}, f32[36,128]{1,0:T(8,128)S(1)}, u32[]{:S(2)}, u32[]{:S(2)}) collective-permute-start(f32[36,128]{1,0:T(8,128)S(1)} %pad_maximum_fusion.refs_0_), channel_id=1, source_target_pairs={{0,16},{8,24},{16,0},{24,8},{1,17},{9,25},{17,1},{25,9},{2,18},{10... | collective-permute-start | bytes 55304 | tf_op jit(solution)/shard_map/ppermute | solution.py:24
  7.1 5.6 %collective-permute-start = (f32[36,128]{1,0:T(8,128)S(1)}, f32[36,128]{1,0:T(8,128)S(1)}, u32[]{:S(2)}, u32[]{:S(2)}) collective-permute-start(f32[36,128]{1,0:T(8,128)S(1)} %pad_maximum_fusion.refs_0_), channel_id=1, source_target_pairs={{0,8},{8,16},{16,24},{24,0},{1,9},{9,17},{17,25},{25,1},{2,10},{10... | collective-permute-start | bytes 55304 | tf_op jit(solution)/shard_map/ppermute | solution.py:24
  8.6 6.4 %copy-start.2 = (f32[36,128]{1,0:T(8,128)}, f32[36,128]{1,0:T(8,128)S(1)}, u32[]{:S(2)}) copy-start(f32[36,128]{1,0:T(8,128)S(1)} %collective-permute-done.2.refs_3_) | copy-start | bytes 55300
  11.8 3.2 %copy-start.3 = (f32[36,128]{1,0:T(8,128)}, f32[36,128]{1,0:T(8,128)S(1)}, u32[]{:S(2)}) copy-start(f32[36,128]{1,0:T(8,128)S(1)} %collective-permute-done.1.refs_2_) | copy-start | bytes 55300
  12.7 2.3 %copy-start.4 = (f32[36,128]{1,0:T(8,128)}, f32[36,128]{1,0:T(8,128)S(1)}, u32[]{:S(2)}) copy-start(f32[36,128]{1,0:T(8,128)S(1)} %collective-permute-done.refs_1_) | copy-start | bytes 55300
  13.4 10.8 %copy-start.1 = (f32[4,512]{1,0:T(4,128)}, f32[4,512]{1,0:T(4,128)S(1)}, u32[]{:S(2)}) copy-start(f32[4,512]{1,0:T(4,128)S(1)} %pad_maximum_fusion.1.refs_3_) | copy-start | bytes 24580
  13.4 10.8 %collective-permute-start.3 = (f32[4,512]{1,0:T(4,128)S(1)}, f32[4,512]{1,0:T(4,128)S(1)}, u32[]{:S(2)}, u32[]{:S(2)}) collective-permute-start(f32[4,512]{1,0:T(4,128)S(1)} %pad_maximum_fusion.1.refs_3_), channel_id=1, source_target_pairs={{0,4},{4,0},{1,5},{5,1},{2,6},{6,2},{3,7},{7,3},{8,12},{12,8},{9,1... | collective-permute-start | bytes 24584 | tf_op jit(solution)/shard_map/ppermute | solution.py:24
  24.2 0.6 copy-start.5

commit v4 on v3

--- a/solution.py
+++ b/solution.py
@@ -15,7 +15,7 @@
 LEAD = SINE[3]
 POLY = tuple(c / LEAD for c in SINE[:3])
 VMEM_LIMIT = 58 * 1024 * 1024
-FACTOR_BLOCK, FACTOR_GROUP, FACTOR_PARTS = 32, 8, 4
+FACTOR_BLOCK, FACTOR_GROUP, FACTOR_SLAB = 32, 4, 32
 
 
 def rotated(x, axis):
@@ -42,73 +42,90 @@
     )
 
 
-def factor_panel(t, first, last, group):
-    row = lax.broadcasted_iota(jnp.int32, t.shape, 0)
-    for j in range(first, last, group):
-        span = range(group)
-        cols = [jnp.broadcast_to(t[:, j + k : j + k + 1], t.shape) for k in span]
-        rows = [t[j + k : j + k + 1, :] for k in span]
-        pivot = [[cols[l][j + k : j + k + 1, :] for l in span] for k in span]
+def reciprocal(x):
+    r = pl.reciprocal(x, approx=True)
+    r = r * (2.0 - x * r)
+    return r * (2.0 - x * r)
+
+
+def factor_panel(t, size, group):
+    depth = t[0].shape[0]
+    row = lax.broadcasted_iota(jnp.int32, t[0].shape, 0)
+    span = range(group)
+    for j in range(0, size, group):
+        top, at = divmod(j, depth)
+        cols = [
+            [jnp.broadcast_to(x[:, j + k : j + k + 1], x.shape) for x in t[top:]] for k in span
+        ]
+        rows = [t[top][at + k : at + k + 1, :] for k in span]
+        yield
+        pivot = [[cols[l][0][at + k : at + k + 1, :] for l in span] for k in span]
         done = []
+        for a in range(0, group, 2):
+            b = a + 1
+            p, q, r = pivot[a][a], pivot[a][b], pivot[b][b]
+            det = p * r - q * q
+            inv = reciprocal(det)
+            yield
+            paa, pab, pbb = r * inv, -(q * inv), p * inv
+            wa = paa * rows[a] + pab * rows[b]
+            wb = pab * rows[a] + pbb * rows[b]
+            for l in range(b + 1, group):
+                fa = paa * pivot[a][l] + pab * pivot[b][l]
+                fb = pab * pivot[a][l] + pbb * pivot[b][l]
+                la, lb = pivot[l][a], pivot[l][b]
+                rows[l] = rows[l] - (la * wa + lb * wb)
+                cols[l] = [x - (y * fa + z * fb) for x, y, z in zip(cols[l], cols[a], cols[b])]
+                for m in range(b + 1, group):
+                    if m <= l:
+                        ma, mb = pivot[m][a], pivot[m][b]
+                        pivot[m][l] = pivot[m][l] - (ma * fa + mb * fb)
+                        pivot[l][m] = pivot[m][l]
+            root = lax.rsqrt(p)
+            done.append(rows[a] * root)
+            done.append((rows[b] - (q * root * root) * rows[a]) * lax.rsqrt(det * root * root))
+            for s, (ca, cb) in enumerate(zip(cols[a], cols[b])):
+                change = ca * wa + cb * wb
+                if s == 0:
+                    change = jnp.where(row >= at + group, change, 0.0)
+                t[top + s] = t[top + s] - change
+            yield
         for k in span:
-            root = lax.rsqrt(pivot[k][k])
-            inverse = root * root
-            weight = rows[k] * inverse
-            for l in range(k + 1, group):
-                lower = pivot[l][k]
-                rows[l] = rows[l] - lower * weight
-                cols[l] = cols[l] - cols[k] * (pivot[k][l] * inverse)
-                for q in range(k + 1, group):
-                    pivot[l][q] = pivot[l][q] - lower * (pivot[k][q] * inverse)
-            t = t - jnp.where(row >= j + group, cols[k], 0.0) * weight
-            done.append(rows[k] * root)
-        for k in span:
-            t = jnp.where(row == j + k, done[k], t)
-    return t
-
-
-def factor_steps(m_ref, k, size, group, parts):
+            t[top] = jnp.where(row == at + k, done[k], t[top])
+    return jnp.concatenate(t, axis=0) if len(t) > 1 else t[0]
+
+
+def factor_step(m_ref, k, size, group):
     n = m_ref.shape[0]
     active = k < n // size
     here = pl.ds(pl.multiple_of(jnp.minimum(k, n // size - 1) * size, size), size)
-    held = {}
 
     def ids(shape):
         return [lax.broadcasted_iota(jnp.int32, shape, d) for d in (0, 1)]
 
-    def begin():
-        row, lane = ids((size, 128))
-        panel = m_ref[here, :]
-        held["t"] = jnp.where(
-            lane < size, panel[:, :128], jnp.where(lane - size == row, 1.0, 0.0)
-        )
-
-    def eliminate(first, last):
-        def run():
-            held["t"] = factor_panel(held["t"], first, last, group)
-        return run
-
-    def solve():
-        row, lane = ids((size, 128))
-        panel = m_ref[here, :]
-        inverse = pltpu.roll(held["t"], 128 - size, 1)[:, :size]
-        head = jnp.where(lane < size, jnp.where(lane == row, 1.0, 0.0), panel[:, :128])
-        held["done"] = dot_f32(inverse, jnp.concatenate([head, panel[:, 128:]], axis=1), 0)
-        low = dot_f32(m_ref[:, :size], inverse, 1)
-        held["low"] = jnp.where(ids((n, size))[0] >= (k + 1) * size, low, 0.0)
-
-    def update():
-        full = m_ref[...]
-        row, lane = ids((n, n))
-        new = jnp.where(lane < size, 0.0, full) - dot_f32(held["low"], held["done"], 0)
-        panel = m_ref[here, :]
-        m_ref[...] = jnp.where(active, pltpu.roll(new, n - size, 1), full)
-        m_ref[here, :] = jnp.where(active, pltpu.roll(held["done"], n - size, 1), panel)
-
-    pieces = [begin]
-    for p in range(parts):
-        pieces.append(eliminate(p * size // parts, (p + 1) * size // parts))
-    return pieces + [solve, update]
+    row, lane = ids((size, 128))
+    t = jnp.where(lane < size, m_ref[here, :128], jnp.where(lane - size == row, 1.0, 0.0))
+    t = yield from factor_panel(
+        [t[r : r + FACTOR_SLAB, :] for r in range(0, size, FACTOR_SLAB)], size, group
+    )
+    yield
+    panel = m_ref[here, :]
+    inverse = pltpu.roll(t, 128 - size, 1)[:, :size]
+    head = jnp.where(lane < size, jnp.where(lane == row, 1.0, 0.0), panel[:, :128])
+    yield
+    done = dot_f32(inverse, jnp.concatenate([head, panel[:, 128:]], axis=1), 0)
+    yield
+    low = dot_f32(m_ref[:, :size], inverse, 1)
+    yield
+    low = jnp.where(ids((n, size))[0] >= (k + 1) * size, low, 0.0)
+    change = dot_f32(low, done, 0)
+    for r in range(0, n, 32):
+        yield
+        full = m_ref[r : r + 32, :]
+        new = jnp.where(ids((32, n))[1] < size, 0.0, full) - change[r : r + 32, :]
+        m_ref[r : r + 32, :] = jnp.where(active, pltpu.roll(new, n - size, 1), full)
+    yield
+    m_ref[here, :] = jnp.where(active, pltpu.roll(done, n - size, 1), panel)
 
 
 def fill_phases(mine, parts_refs, sums_ref, pt_ref):
@@ -241,6 +258,8 @@
     first_row = pl.multiple_of(mine * rows, rows)
     first_col = pl.multiple_of(lax.axis_index("pcol") * cols, cols)
     segments = [(0, rows), (rows + lead, width)]
+    chunks = [(at, min(at + 256, stop)) for start, stop in segments for at in range(start, stop, 256)]
+    n_lead_chunks = -(-rows // 256)
 
     def design(start, row):
         def run():
@@ -265,7 +284,7 @@
     def products(f_ref):
         pieces = [(0, lead, rows)]
         pieces += [(c, min(c + 256, lead + cols), rows + lead) for c in range(lead, lead + cols, 256)]
-        return [product(f_ref, *piece) for piece in pieces]
+        return [(product(f_ref, *p), (p[1] - p[0]) * p[2] * tile) for p in pieces]
 
     @pl.when(step == 0)
     def _():
@@ -273,7 +292,6 @@
         r_ref[...] = table
         h_ref[:rows, :] = r_ref[pl.ds(first_row, rows), :]
         h_ref[rows + lead :, :] = r_ref[pl.ds(first_col, cols), :]
-        fb_ref[...] = jnp.zeros_like(fb_ref)
         acc_ref[...] = jnp.zeros_like(acc_ref)
         d_ref[...] = jnp.zeros_like(d_ref)
         n_epoch = held_refs[0].shape[0]
@@ -294,33 +312,46 @@
             for row in range(begin, end, 16):
                 design(0, row)()
 
-    def phase(f_ref, before_ref, half, extra):
+    def phase(f_ref, half, extra):
         following = pl.multiple_of(lax.rem((2 * step + half + 1) * tile, epochs), tile)
         f_ref[rows : rows + lead, :] = lead_ref[:, half * tile : (half + 1) * tile]
-        chunk = 256
-        sets = []
-        for start, stop in segments:
-            for at in range(start, stop, chunk):
-                sets.append((at, min(at + chunk, stop)))
-        later = products(before_ref)
-        for k, (at, end) in enumerate(sets):
+        work, ready = [], []
+
+        def filters(begin, end):
             for b in range(tile // count):
-                filtered(f_ref, at, end, b)()
-            for n in range(k * len(later) // len(sets), (k + 1) * len(later) // len(sets)):
-                later[n]()
-            for row in range(at, end, 16):
-                design(following, row)()
-            for n in range(k * len(extra) // len(sets), (k + 1) * len(extra) // len(sets)):
-                extra[n]()
-
-    pieces = factor_steps(m_ref, step, FACTOR_BLOCK, FACTOR_GROUP, FACTOR_PARTS)
-    phase(fa_ref, fb_ref, 0, pieces[: len(pieces) // 2])
-    phase(fb_ref, fa_ref, 1, pieces[len(pieces) // 2 :])
+                work.append((filtered(f_ref, begin, end, b), (end - begin) * 2 * count * count, None))
+            work[-1] = (*work[-1][:2], range(begin, end, 16))
+
+        pieces = products(f_ref)
+        for begin, end in chunks[:n_lead_chunks]:
+            filters(begin, end)
+        for n, (begin, end) in enumerate(chunks[n_lead_chunks:]):
+            filters(begin, end)
+            work.append((*pieces[n], None))
+        for piece in pieces[len(chunks) - n_lead_chunks :]:
+            work.append((*piece, None))
+        total, spent, given = sum(w[1] for w in work), 0, 0
+        every = sum(end - begin for begin, end in chunks) // 16
+        for run, cost, rows_done in work:
+            run()
+            spent += cost
+            ready += list(rows_done or ())
+            while given < every * spent // total and ready:
+                design(following, ready.pop(0))()
+                next(extra, None)
+                given += 1
+        for row in ready:
+            design(following, row)()
+            next(extra, None)
+
+    factor = factor_step(m_ref, step, FACTOR_BLOCK, FACTOR_GROUP)
+    phase(fa_ref, 0, factor)
+    phase(fb_ref, 1, factor)
+    for _ in factor:
+        pass
 
     @pl.when(step == pl.num_programs(0) - 1)
     def _():
-        for run in products(fb_ref):
-            run()
         mid = -(-rows // 128) * 128
         own = ridge_ref[...]
         if mid > rows:
@@ -340,8 +371,8 @@
 
         @pl.loop(epochs // (2 * tile), max(lead // FACTOR_BLOCK, epochs // (2 * tile)))
         def _(k):
-            for run in factor_steps(m_ref, k, FACTOR_BLOCK, FACTOR_GROUP, FACTOR_PARTS):
-                run()
+            for _ in factor_step(m_ref, k, FACTOR_BLOCK, FACTOR_GROUP):
+                pass
 
         inverse = jnp.where(i >= j, m_ref[...], 0.0)
         highest = functools.partial(

time: 82 us -> 77.6 us (0.946)
  Pallas kernels: 66.1 us -> 61.7 us
    pallas_call x1, Pallas kernels: 56.9 us -> 52.5 us  [on_device(): pl.pallas_call(functools.partial(main_kernel, (rows, B, cols, n_row)), gr...]
  transfers between devices with their start and end apart: 4 -> 4, of which waited for: 3 -> 3; matrix products, arithmetic and copies ran while one was open for 0% -> 0% of each run, Pallas kernels for 11% -> 12%
where the time goes in v4:
time: 77.6 us; the launch traced here: 77.3 us
  Pallas kernels  61.7 us (80%)
  starting transfers between devices  7.62 us (10%)
  waiting for transfers between devices  4.56 us (6%)
  other arithmetic  2.12 us (3%)
    pallas_call x1, Pallas kernels, on_device(): pl.pallas_call(functools.partial(main_kernel, (rows, B, cols, n_row)), gr...  52.5 us
    pallas_call x1, Pallas kernels, on_device(): pl.pallas_call(functools.partial(lead_kernel, len(parts)), grid=(epochs /...  9.18 us
    ppermute x4, starting transfers between devices, rotated(): return [x] + [lax.ppermute(x, axis, pairs) for pairs in shifts]  7.62 us
    ppermute x4, waiting for transfers between devices, rotated(): return [x] + [lax.ppermute(x, axis, pairs) for pairs in shifts]  4.56 us
  transfers between devices with their start and end apart: 4, of which 3 were waited for; matrix products, arithmetic and copies ran while one was open for 0% of the time, Pallas kernels for 12%

profile of v4, /device:TPU:0, one launch (start us, length us, event | category | flops | bytes accessed | tf_op | source)
XLA Modules:
  0.0 77.3 jit_solution(1008024706786780671)
XLA Ops:
  0.6 0.7 convert_element_type.3
  1.4 0.7 pad_maximum_fusion.refs_0_
  2.1 0.0 copy-start
  2.1 5.0 %collective-permute-start.2 = (f32[36,128]{1,0:T(8,128)S(1)}, f32[36,128]{1,0:T(8,128)S(1)}, u32[]{:S(2)}, u32[]{:S(2)}) collective-permute-start(f32[36,128]{1,0:T(8,128)S(1)} %pad_maximum_fusion.refs_0_), channel_id=1, source_target_pairs={{0,24},{8,0},{16,8},{24,16},{1,25},{9,1},{17,9},{25,17},{2,26},{10... | collective-permute-start | bytes 55304 | tf_op jit(solution)/shard_map/ppermute | solution.py:24
  7.1 0.0 collective-permute-start.1
  7.1 1.0 %collective-permute-start = (f32[36,128]{1,0:T(8,128)S(1)}, f32[36,128]{1,0:T(8,128)S(1)}, u32[]{:S(2)}, u32[]{:S(2)}) collective-permute-start(f32[36,128]{1,0:T(8,128)S(1)} %pad_maximum_fusion.refs_0_), channel_id=1, source_target_pairs={{0,8},{8,16},{16,24},{24,0},{1,9},{9,17},{17,25},{25,1},{2,10},{10... | collective-permute-start | bytes 55304 | tf_op jit(solution)/shard_map/ppermute | solution.py:24
  8.1 0.5 collective-permute-done.2.refs_3_
  8.6 0.0 copy-start.2
  8.6 3.2 %collective-permute-done.1.refs_2_ = f32[36,128]{1,0:T(8,128)S(1)} collective-permute-done((f32[36,128]{1,0:T(8,128)S(1)}, f32[36,128]{1,0:T(8,128)S(1)}, u32[]{:S(2)}, u32[]{:S(2)}) %collective-permute-start.1) | collective-permute-done | bytes 18464 | tf_op jit(solution)/shard_map/ppermute | solution.py:24
  11.8 0.0 copy-start.3
  11.8 0.9 %collective-permute-done.refs_1_ = f32[36,128]{1,0:T(8,128)S(1)} collective-permute-done((f32[36,128]{1,0:T(8,128)S(1)}, f32[36,128]{1,0:T(8,128)S(1)}, u32[]{:S(2)}, u32[]{:S(2)}) %collective-permute-start) | collective-permute-done | bytes 18464 | tf_op jit(solution)/shard_map/ppermute | solution.py:24
  12.7 0.0 copy-start.4
  12.7 0.7 pad_maximum_fusion.1.refs_3_
  13.4 0.0 copy-start.1
  13.4 1.6 %collective-permute-start.3 = (f32[4,512]{1,0:T(4,128)S(1)}, f32[4,512]{1,0:T(4,128)S(1)}, u32[]{:S(2)}, u32[]{:S(2)}) collective-permute-start(f32[4,512]{1,0:T(4,128)S(1)} %pad_maximum_fusion.1.refs_3_), channel_id=1, source_target_pairs={{0,4},{4,0},{1,5},{5,1},{2,6},{6,2},{3,7},{7,3},{8,12},{12,8},{9,1... | collective-permute-start | bytes 24584 | tf_op jit(solution)/shard_map/ppermute | solution.py:24
  15.0 0.0 copy-done
  15.0 0.0 copy-done.2
  15.0 0.0 copy-done.3
  15.0 0.0 copy-done.4
  15.0 9.2 %shard_map.68 = (f32[8,8192]{1,0:T(8,128)}, bf16[512,256]{1,0:T(8,128)(2,1)}, bf16[256,8192]{1,0:T(8,128)(2,1)}, f32[256,256]{1,0:T(8,128)}) custom-call(f32[36,128]{1,0:T(8,128)} %copy-done, f32[36,128]{1,0:T(8,128)} %copy-done.4, f32[36,128]{1,0:T(8,128)} %copy-done.3, f32[36,128]{1,0:T(8,128)} %copy-done.2, s32[1,4096]{1,0:T(1,128)} %bitcast.8, ...), custom_call_target="tpu_custom_call" | custom-call | tf_op jit(solution)/shard_map/pallas_call | solution.py:417
  24.2 0.0 collective-permute-done.3.refs_4_
  24.2 0.0 copy-start.5
  24.2 0.0 copy-done.1
  24.2 0.6 copy-done.5
  24.8 52.5 %shard_map.69 = (f32[512,256]{1,0:T(8,128)}, f32[512,1024]{1,0:T(8,128)}) custom-call(s32[1,4096]{1,0:T(1,128)} %bitcast.9, f32[1,4096]{1,0:T(1,128)} %bitcast.11, f32[1,512]{1,0:T(1,128)} %bitcast.14, f32[4,512]{1,0:T(4,128)} %copy-done.1, f32[4,512]{1,0:T(4,128)} %copy-done.5, f32[8,8192]{1,0:T(8,128)} %get-tuple-element.6.refs_5_, ...), custom_call_target="tpu_custom_call" | custom-call | tf_op jit(solution)/shard_map/pallas_call | solution.py:431
  (4 shorter events, 0.0 us)
Async XLA Ops:
  2.1 12.9 %copy-start = (f32[36,128]{1,0:T(8,128)}, f32[36,128]{1,0:T(8,128)S(1)}, u32[]{:S(2)}) copy-start(f32[36,128]{1,0:T(8,128)S(1)} %pad_maximum_fusion.refs_0_) | copy-start | bytes 55300
  2.1 6.5 %collective-permute-start.2 = (f32[36,128]{1,0:T(8,128)S(1)}, f32[36,128]{1,0:T(8,128)S(1)}, u32[]{:S(2)}, u32[]{:S(2)}) collective-permute-start(f32[36,128]{1,0:T(8,128)S(1)} %pad_maximum_fusion.refs_0_), channel_id=1, source_target_pairs={{0,24},{8,0},{16,8},{24,16},{1,25},{9,1},{17,9},{25,17},{2,26},{10... | collective-permute-start | bytes 55304 | tf_op jit(solution)/shard_map/ppermute | solution.py:24
  7.1 4.7 %collective-permute-start.1 = (f32[36,128]{1,0:T(8,128)S(1)}, f32[36,128]{1,0:T(8,128)S(1)}, u32[]{:S(2)}, u32[]{:S(2)}) collective-permute-start(f32[36,128]{1,0:T(8,128)S(1)} %pad_maximum_fusion.refs_0_), channel_id=1, source_target_pairs={{0,16},{8,24},{16,0},{24,8},{1,17},{9,25},{17,1},{25,9},{2,18},{10... | collective-permute-start | bytes 55304 | tf_op jit(solution)/shard_map/ppermute | solution.py:24
  7.1 5.6 %collective-permute-start = (f32[36,128]{1,0:T(8,128)S(1)}, f32[36,128]{1,0:T(8,128)S(1)}, u32[]{:S(2)}, u32[]{:S(2)}) collective-permute-start(f32[36,128]{1,0:T(8,128)S(1)} %pad_maximum_fusion.refs_0_), channel_id=1, source_target_pairs={{0,8},{8,16},{16,24},{24,0},{1,9},{9,17},{17,25},{25,1},{2,10},{10... | collective-permute-start | bytes 55304 | tf_op jit(solution)/shard_map/ppermute | solution.py:24
  8.6 6.4 %copy-start.2 = (f32[36,128]{1,0:T(8,128)}, f32[36,128]{1,0:T(8,128)S(1)}, u32[]{:S(2)}) copy-start(f32[36,128]{1,0:T(8,128)S(1)} %collective-permute-done.2.refs_3_) | copy-start | bytes 55300
  11.8 3.2 %copy-start.3 = (f32[36,128]{1,0:T(8,128)}, f32[36,128]{1,0:T(8,128)S(1)}, u32[]{:S(2)}) copy-start(f32[36,128]{1,0:T(8,128)S(1)} %collective-permute-done.1.refs_2_) | copy-start | bytes 55300
  12.7 2.3 %copy-start.4 = (f32[36,128]{1,0:T(8,128)}, f32[36,128]{1,0:T(8,128)S(1)}, u32[]{:S(2)}) copy-start(f32[36,128]{1,0:T(8,128)S(1)} %collective-permute-done.refs_1_) | copy-start | bytes 55300
  13.4 10.8 %copy-start.1 = (f32[4,512]{1,0:T(4,128)}, f32[4,512]{1,0:T(4,128)S(1)}, u32[]{:S(2)}) copy-start(f32[4,512]{1,0:T(4,128)S(1)} %pad_maximum_fusion.1.refs_3_) | copy-start | bytes 24580
  13.4 10.8 %collective-permute-start.3 = (f32[4,512]{1,0:T(4,128)S(1)}, f32[4,512]{1,0:T(4,128)S(1)}, u32[]{:S(2)}, u32[]{:S(2)}) collective-permute-start(f32[4,512]{1,0:T(4,128)S(1)} %pad_maximum_fusion.1.refs_3_), channel_id=1, source_target_pairs={{0,4},{4,0},{1,5},{5,1},{2,6},{6,2},{3,7},{7,3},{8,12},{12,8},{9,1... | collective-permute-start | bytes 24584 | tf_op jit(solution)/shard_map/ppermute | solution.py:24
  24.2 0.6 copy-start.5

commit v5 on v4

--- a/solution.py
+++ b/solution.py
@@ -134,7 +134,9 @@
     blocks = each // 2
     for k, ref in enumerate(parts_refs):
         group = lax.rem(mine - k + count, count)
-        sums_ref[pl.ds(pl.multiple_of(group * each, each), each), :] = ref[:each, :]
+        lanes = [ref[a : a + 1, b * 128 : (b + 1) * 128] for a in range(2) for b in range(blocks)]
+        rows = pl.ds(pl.multiple_of(group * each, each), each)
+        sums_ref[rows, :] = jnp.concatenate(lanes, axis=0)
     total = sums_ref.shape[0]
     terms = sums_ref[...].astype(jnp.bfloat16)
     i = lax.broadcasted_iota(jnp.int32, (128, 128), 0)
@@ -204,15 +206,13 @@
     ).astype(jnp.bfloat16)
 
 
-def lead_kernel(n_parts, *refs):
-    parts_refs = refs[:n_parts]
-    harmonic_ref, scale_ref, taps_ref = refs[n_parts : n_parts + 3]
-    pt_ref, wt_ref, lead_ref, block_ref = refs[n_parts + 3 : n_parts + 7]
-    sums_ref, h_ref, d_ref = refs[n_parts + 7 :]
-    lead, tile = lead_ref.shape
+def fill_lead(h_ref, pt_ref, wt_ref, d_ref, lead_ref, block_ref):
+    tiles, lead, tile = lead_ref.shape
     epochs = pt_ref.shape[1]
     count = wt_ref.shape[1]
-    step = pl.program_id(0)
+    blocks = tile // count
+    d_ref[:, :count] = jnp.zeros((lead, count), jnp.bfloat16)
+    block_ref[...] = jnp.zeros_like(block_ref)
 
     def design(start, block):
         for row in range(0, lead, 16):
@@ -220,36 +220,32 @@
                 h_ref, pt_ref, d_ref, row, row + 16, (block + 1) * count, start + block * count
             )
 
-    @pl.when(step == 0)
-    def _():
-        fill_phases(lax.axis_index("epoch"), parts_refs, sums_ref, pt_ref)
-        fill_toeplitz(taps_ref, wt_ref)
-        h_ref[...] = parameter_table(harmonic_ref[:, :lead], scale_ref[:, :lead])
-        d_ref[:, :count] = jnp.zeros((lead, count), jnp.bfloat16)
-        block_ref[...] = jnp.zeros_like(block_ref)
-        for b in range(tile // count):
-            design(0, b)
-
-    following = pl.multiple_of(lax.rem((step + 1) * tile, epochs), tile)
-    blocks = tile // count
     for b in range(blocks):
-        fill_filtered(d_ref, wt_ref, lead_ref, 0, lead, b)
-        if b == min(1, blocks - 1):
-            d_ref[:, :count] = d_ref[:, tile:]
-        if b > 0:
-            design(following, b - 1)
-    design(following, blocks - 1)
-    block_ref[...] += lax.dot_general(
-        lead_ref[...], lead_ref[...], (((1,), (1,)), ((), ())), preferred_element_type=jnp.float32
-    )
+        design(0, b)
+
+    @pl.loop(0, tiles)
+    def _(step):
+        following = pl.multiple_of(lax.rem((step + 1) * tile, epochs), tile)
+        out_ref = lead_ref.at[step]
+        for b in range(blocks):
+            fill_filtered(d_ref, wt_ref, out_ref, 0, lead, b)
+            if b == min(1, blocks - 1):
+                d_ref[:, :count] = d_ref[:, tile:]
+            if b > 0:
+                design(following, b - 1)
+        design(following, blocks - 1)
+        block_ref[...] += lax.dot_general(
+            out_ref[...], out_ref[...], (((1,), (1,)), ((), ())), preferred_element_type=jnp.float32
+        )
 
 
 def main_kernel(shape, *refs):
-    rows, lead, cols, n_row = shape
-    harmonic_ref, scale_ref, ridge_ref = refs[:3]
-    held_refs = refs[3 : 3 + n_row]
-    pt_ref, wt_ref, lead_ref, block_ref = refs[3 + n_row : 7 + n_row]
-    panel_ref, schur_ref, h_ref, r_ref, d_ref, fa_ref, fb_ref, acc_ref, m_ref, first_ref = refs[7 + n_row :]
+    rows, lead, cols, n_epoch, n_row = shape
+    parts_refs, refs = refs[:n_epoch], refs[n_epoch:]
+    held_refs, refs = refs[:n_row], refs[n_row:]
+    harmonic_ref, scale_ref, taps_ref, ridge_ref, panel_ref, schur_ref = refs[:6]
+    sums_ref, pt_ref, wt_ref, dl_ref, lead_ref, block_ref = refs[6:12]
+    h_ref, r_ref, d_ref, fa_ref, fb_ref, acc_ref, m_ref, first_ref = refs[12:]
     width, tile = fa_ref.shape
     count = wt_ref.shape[1]
     step = pl.program_id(0)
@@ -288,13 +284,14 @@
 
     @pl.when(step == 0)
     def _():
-        table = parameter_table(harmonic_ref[...], scale_ref[...])
-        r_ref[...] = table
+        fill_phases(lax.axis_index("epoch"), parts_refs, sums_ref, pt_ref)
+        fill_toeplitz(taps_ref, wt_ref)
+        r_ref[...] = parameter_table(harmonic_ref[...], scale_ref[...])
+        fill_lead(r_ref, pt_ref, wt_ref, dl_ref, lead_ref, block_ref)
         h_ref[:rows, :] = r_ref[pl.ds(first_row, rows), :]
         h_ref[rows + lead :, :] = r_ref[pl.ds(first_col, cols), :]
         acc_ref[...] = jnp.zeros_like(acc_ref)
         d_ref[...] = jnp.zeros_like(d_ref)
-        n_epoch = held_refs[0].shape[0]
         first = []
         for q in range(-(-lead // rows)):
             for k, ref in enumerate(held_refs):
@@ -314,7 +311,7 @@
 
     def phase(f_ref, half, extra):
         following = pl.multiple_of(lax.rem((2 * step + half + 1) * tile, epochs), tile)
-        f_ref[rows : rows + lead, :] = lead_ref[:, half * tile : (half + 1) * tile]
+        f_ref[rows : rows + lead, :] = lead_ref[step, :, half * tile : (half + 1) * tile]
         work, ready = [], []
 
         def filters(begin, end):
@@ -397,53 +394,37 @@
     epochs = steps.shape[1] * n_epoch
     count = taps.shape[0]
     tile = 512
-    lead_tile = 1024
-    step_rows = 2 * steps.shape[1] // 128
-    ridge_rows = -(-rows // 128)
-    packed = jnp.concatenate(
-        [
-            steps.astype(jnp.float32).reshape(step_rows, 128),
-            jnp.pad(ridge, (0, ridge_rows * 128 - rows)).reshape(ridge_rows, 128),
-        ]
-    )
-    parts = rotated(packed, "epoch")
-    held = jnp.stack([x[step_rows:].reshape(-1) for x in parts])
-    held = rotated(held, "prow")
+    here = steps.shape[1]
+    ridge_rows = -(-rows // here)
+    ridge_part = jnp.pad(ridge, (0, ridge_rows * here - rows)).reshape(ridge_rows, here)
+    parts = rotated(jnp.concatenate([steps.astype(jnp.float32), ridge_part]), "epoch")
+    held = rotated(jnp.stack([x[2:, : min(rows, here)].reshape(-1) for x in parts]), "prow")
     row_of = lambda x: x.reshape(1, -1)
     in_vmem = pl.BlockSpec(memory_space=pltpu.VMEM)
     f32 = lambda *shape: jax.ShapeDtypeStruct(shape, jnp.float32)
-    bf16 = lambda *shape: jax.ShapeDtypeStruct(shape, jnp.bfloat16)
-    params_row, scales_row = row_of(harmonic), row_of(col_scale)
-    shared = pl.pallas_call(
-        functools.partial(lead_kernel, len(parts)),
-        grid=(epochs // lead_tile,),
-        out_shape=(f32(8, epochs), bf16(2 * count, count), bf16(B, epochs), f32(B, B)),
-        in_specs=[in_vmem] * (len(parts) + 3),
-        out_specs=(in_vmem, in_vmem, pl.BlockSpec((B, lead_tile), lambda i: (0, i)), in_vmem),
-        scratch_shapes=[
-            pltpu.VMEM((2 * epochs // 128, 128), jnp.float32),
-            pltpu.VMEM((B, 128), jnp.float32),
-            pltpu.VMEM((B, count + lead_tile), jnp.bfloat16),
-        ],
-        compiler_params=pltpu.CompilerParams(vmem_limit_bytes=VMEM_LIMIT),
-    )(*parts, params_row, scales_row, row_of(taps))
-    operands = (params_row, scales_row, row_of(ridge), *held, *shared)
+    operands = (*parts, *held, row_of(harmonic), row_of(col_scale), row_of(taps), row_of(ridge))
+    vmem = lambda dtype, *shape: pltpu.VMEM(shape, dtype)
     return pl.pallas_call(
-        functools.partial(main_kernel, (rows, B, cols, n_row)),
+        functools.partial(main_kernel, (rows, B, cols, n_epoch, n_row)),
         grid=(epochs // (2 * tile),),
         out_shape=(f32(rows, B), f32(rows, cols)),
-        in_specs=[in_vmem] * (len(operands) - 2)
-        + [pl.BlockSpec((B, 2 * tile), lambda i: (0, i)), in_vmem],
+        in_specs=[in_vmem] * len(operands),
         out_specs=(in_vmem, in_vmem),
         scratch_shapes=[
-            pltpu.VMEM((width, 128), jnp.float32),
-            pltpu.VMEM((params, 128), jnp.float32),
-            pltpu.VMEM((width, count + tile), jnp.bfloat16),
-            pltpu.VMEM((width, tile), jnp.bfloat16),
-            pltpu.VMEM((width, tile), jnp.bfloat16),
-            pltpu.VMEM((rows + B, B + cols), jnp.float32),
-            pltpu.VMEM((B, B), jnp.float32),
-            pltpu.VMEM((B, 128), jnp.float32),
+            vmem(jnp.float32, 2 * epochs // 128, 128),
+            vmem(jnp.float32, 8, epochs),
+            vmem(jnp.bfloat16, 2 * count, count),
+            vmem(jnp.bfloat16, B, count + 2 * tile),
+            vmem(jnp.bfloat16, epochs // (2 * tile), B, 2 * tile),
+            vmem(jnp.float32, B, B),
+            vmem(jnp.float32, width, 128),
+            vmem(jnp.float32, params, 128),
+            vmem(jnp.bfloat16, width, count + tile),
+            vmem(jnp.bfloat16, width, tile),
+            vmem(jnp.bfloat16, width, tile),
+            vmem(jnp.float32, rows + B, B + cols),
+            vmem(jnp.float32, B, B),
+            vmem(jnp.float32, B, 128),
         ],
         compiler_params=pltpu.CompilerParams(vmem_limit_bytes=VMEM_LIMIT),
     )(*operands)

time: 77.6 us -> 76.5 us (0.986)
  Pallas kernels: 61.7 us -> 59 us
  waiting for transfers between devices: 4.56 us -> 6.84 us
  other arithmetic: 2.12 us -> 0.76 us
    pallas_call x2 -> x1, Pallas kernels: 61.7 us -> 59 us  [on_device(): pl.pallas_call(functools.partial(main_kernel, (rows, B, cols, n_epoch, n_...]
    ppermute x4, waiting for transfers between devices: 4.56 us -> 6.84 us  [rotated(): return [x] + [lax.ppermute(x, axis, pairs) for pairs in shifts]]
  transfers between devices with their start and end apart: 4 -> 4, of which waited for: 3 -> 4; matrix products, arithmetic and copies ran while one was open for 0% -> 0% of each run, Pallas kernels for 12% -> 0%
where the time goes in v5:
time: 76.5 us; the launch traced here: 76.2 us
  Pallas kernels  59 us (77%)
  starting transfers between devices  7.67 us (10%)
  waiting for transfers between devices  6.84 us (9%)
  local copies, waits for them, and re-layouts  1.28 us (2%)
    pallas_call x1, Pallas kernels, on_device(): pl.pallas_call(functools.partial(main_kernel, (rows, B, cols, n_epoch, n_...  59 us
    ppermute x4, starting transfers between devices, rotated(): return [x] + [lax.ppermute(x, axis, pairs) for pairs in shifts]  7.67 us
    ppermute x4, waiting for transfers between devices, rotated(): return [x] + [lax.ppermute(x, axis, pairs) for pairs in shifts]  6.84 us
  transfers between devices with their start and end apart: 4, of which 4 were waited for; matrix products, arithmetic and copies ran while one was open for 0% of the time, Pallas kernels for 0%

profile of v5, /device:TPU:0, one launch (start us, length us, event | category | flops | bytes accessed | tf_op | source)
XLA Modules:
  0.0 76.2 jit_solution(12763610513660217947)
XLA Ops:
  0.6 0.7 convert_element_type.5
  1.4 0.7 pad.4
  2.1 0.0 copy-start
  2.1 5.1 %collective-permute-start.2 = (f32[3,2048]{1,0:T(4,128)S(1)}, f32[3,2048]{1,0:T(4,128)S(1)}, u32[]{:S(2)}, u32[]{:S(2)}) collective-permute-start(f32[3,2048]{1,0:T(4,128)S(1)} %pad_maximum_fusion.refs_0_), channel_id=1, source_target_pairs={{0,24},{8,0},{16,8},{24,16},{1,25},{9,1},{17,9},{25,17},{2,26},{10... | collective-permute-start | bytes 73736 | tf_op jit(solution)/shard_map/ppermute | solution.py:24
  7.2 0.0 collective-permute-start.1
  7.2 1.0 %collective-permute-start = (f32[3,2048]{1,0:T(4,128)S(1)}, f32[3,2048]{1,0:T(4,128)S(1)}, u32[]{:S(2)}, u32[]{:S(2)}) collective-permute-start(f32[3,2048]{1,0:T(4,128)S(1)} %pad_maximum_fusion.refs_0_), channel_id=1, source_target_pairs={{0,8},{8,16},{16,24},{24,0},{1,9},{9,17},{17,25},{25,1},{2,10},{10... | collective-permute-start | bytes 73736 | tf_op jit(solution)/shard_map/ppermute | solution.py:24
  8.2 0.6 collective-permute-done.2.refs_3_
  8.8 0.0 copy-start.1
  8.8 3.2 %collective-permute-done.1.refs_2_ = f32[3,2048]{1,0:T(4,128)S(1)} collective-permute-done((f32[3,2048]{1,0:T(4,128)S(1)}, f32[3,2048]{1,0:T(4,128)S(1)}, u32[]{:S(2)}, u32[]{:S(2)}) %collective-permute-start.1) | collective-permute-done | bytes 24608 | tf_op jit(solution)/shard_map/ppermute | solution.py:24
  12.0 0.0 copy-start.2
  12.0 0.9 %collective-permute-done.refs_1_ = f32[3,2048]{1,0:T(4,128)S(1)} collective-permute-done((f32[3,2048]{1,0:T(4,128)S(1)}, f32[3,2048]{1,0:T(4,128)S(1)}, u32[]{:S(2)}, u32[]{:S(2)}) %collective-permute-start) | collective-permute-done | bytes 24608 | tf_op jit(solution)/shard_map/ppermute | solution.py:24
  12.9 0.0 copy-start.3
  12.9 0.0 copy-start.4
  12.9 1.6 %collective-permute-start.3 = (f32[4,512]{1,0:T(4,128)S(1)}, f32[4,512]{1,0:T(4,128)S(1)}, u32[]{:S(2)}, u32[]{:S(2)}) collective-permute-start(f32[4,512]{1,0:T(4,128)S(1)} %pad_maximum_fusion.1.refs_4_), channel_id=1, source_target_pairs={{0,4},{4,0},{1,5},{5,1},{2,6},{6,2},{3,7},{7,3},{8,12},{12,8},{9,1... | collective-permute-start | bytes 24584 | tf_op jit(solution)/shard_map/ppermute | solution.py:24
  14.5 2.2 %collective-permute-done.3.refs_5_ = f32[4,512]{1,0:T(4,128)S(1)} collective-permute-done((f32[4,512]{1,0:T(4,128)S(1)}, f32[4,512]{1,0:T(4,128)S(1)}, u32[]{:S(2)}, u32[]{:S(2)}) %collective-permute-start.3) | collective-permute-done | bytes 8224 | tf_op jit(solution)/shard_map/ppermute | solution.py:24
  16.6 0.0 copy-start.5
  16.6 0.0 copy-done
  16.6 0.0 copy-done.1
  16.6 0.0 copy-done.2
  16.7 0.0 copy-done.3
  16.7 0.0 copy-done.4
  16.7 0.6 copy-done.5
  17.2 59.0 %shard_map.68 = (f32[512,256]{1,0:T(8,128)}, f32[512,1024]{1,0:T(8,128)}) custom-call(f32[3,2048]{1,0:T(4,128)} %copy-done, f32[3,2048]{1,0:T(4,128)} %copy-done.3, f32[3,2048]{1,0:T(4,128)} %copy-done.2, f32[3,2048]{1,0:T(4,128)} %copy-done.1, f32[4,512]{1,0:T(4,128)} %copy-done.4, f32[4,512]{1,0:T(4,128)} %copy-done.5, s32[1,4096]{1,0:T(1,128)} %bitcast.7, ...), custom_call_target="tpu_custom_call" | custom-call | tf_op jit(solution)/shard_map/pallas_call | solution.py:407
  (6 shorter events, 0.1 us)
Async XLA Ops:
  2.1 14.6 %copy-start = (f32[3,2048]{1,0:T(4,128)}, f32[3,2048]{1,0:T(4,128)S(1)}, u32[]{:S(2)}) copy-start(f32[3,2048]{1,0:T(4,128)S(1)} %pad_maximum_fusion.refs_0_) | copy-start | bytes 73732
  2.1 6.7 %collective-permute-start.2 = (f32[3,2048]{1,0:T(4,128)S(1)}, f32[3,2048]{1,0:T(4,128)S(1)}, u32[]{:S(2)}, u32[]{:S(2)}) collective-permute-start(f32[3,2048]{1,0:T(4,128)S(1)} %pad_maximum_fusion.refs_0_), channel_id=1, source_target_pairs={{0,24},{8,0},{16,8},{24,16},{1,25},{9,1},{17,9},{25,17},{2,26},{10... | collective-permute-start | bytes 73736 | tf_op jit(solution)/shard_map/ppermute | solution.py:24
  7.2 4.8 %collective-permute-start.1 = (f32[3,2048]{1,0:T(4,128)S(1)}, f32[3,2048]{1,0:T(4,128)S(1)}, u32[]{:S(2)}, u32[]{:S(2)}) collective-permute-start(f32[3,2048]{1,0:T(4,128)S(1)} %pad_maximum_fusion.refs_0_), channel_id=1, source_target_pairs={{0,16},{8,24},{16,0},{24,8},{1,17},{9,25},{17,1},{25,9},{2,18},{10... | collective-permute-start | bytes 73736 | tf_op jit(solution)/shard_map/ppermute | solution.py:24
  7.2 5.7 %collective-permute-start = (f32[3,2048]{1,0:T(4,128)S(1)}, f32[3,2048]{1,0:T(4,128)S(1)}, u32[]{:S(2)}, u32[]{:S(2)}) collective-permute-start(f32[3,2048]{1,0:T(4,128)S(1)} %pad_maximum_fusion.refs_0_), channel_id=1, source_target_pairs={{0,8},{8,16},{16,24},{24,0},{1,9},{9,17},{17,25},{25,1},{2,10},{10... | collective-permute-start | bytes 73736 | tf_op jit(solution)/shard_map/ppermute | solution.py:24
  8.8 7.9 %copy-start.1 = (f32[3,2048]{1,0:T(4,128)}, f32[3,2048]{1,0:T(4,128)S(1)}, u32[]{:S(2)}) copy-start(f32[3,2048]{1,0:T(4,128)S(1)} %collective-permute-done.2.refs_3_) | copy-start | bytes 73732
  12.0 4.7 %copy-start.2 = (f32[3,2048]{1,0:T(4,128)}, f32[3,2048]{1,0:T(4,128)S(1)}, u32[]{:S(2)}) copy-start(f32[3,2048]{1,0:T(4,128)S(1)} %collective-permute-done.1.refs_2_) | copy-start | bytes 73732
  12.9 3.8 %copy-start.3 = (f32[3,2048]{1,0:T(4,128)}, f32[3,2048]{1,0:T(4,128)S(1)}, u32[]{:S(2)}) copy-start(f32[3,2048]{1,0:T(4,128)S(1)} %collective-permute-done.refs_1_) | copy-start | bytes 73732
  12.9 3.8 %copy-start.4 = (f32[4,512]{1,0:T(4,128)}, f32[4,512]{1,0:T(4,128)S(1)}, u32[]{:S(2)}) copy-start(f32[4,512]{1,0:T(4,128)S(1)} %pad_maximum_fusion.1.refs_4_) | copy-start | bytes 24580
  12.9 3.7 %collective-permute-start.3 = (f32[4,512]{1,0:T(4,128)S(1)}, f32[4,512]{1,0:T(4,128)S(1)}, u32[]{:S(2)}, u32[]{:S(2)}) collective-permute-start(f32[4,512]{1,0:T(4,128)S(1)} %pad_maximum_fusion.1.refs_4_), channel_id=1, source_target_pairs={{0,4},{4,0},{1,5},{5,1},{2,6},{6,2},{3,7},{7,3},{8,12},{12,8},{9,1... | collective-permute-start | bytes 24584 | tf_op jit(solution)/shard_map/ppermute | solution.py:24
  16.6 0.6 copy-start.5

commit v6 on v5

--- a/solution.py
+++ b/solution.py
@@ -31,12 +31,22 @@
     return high, mid, (rest - mid.astype(jnp.float32)).astype(jnp.bfloat16)
 
 
-def dot_f32(a, b, b_dim):
+def dot_f32(a, b, a_dim, b_dim):
     ah, am, al = split3(a)
     bh, bm, bl = split3(b)
     return lax.dot_general(
-        jnp.concatenate([ah, ah, am, ah, al, am], axis=1),
+        jnp.concatenate([ah, ah, am, ah, al, am], axis=a_dim),
         jnp.concatenate([bh, bm, bh, bl, bh, bm], axis=b_dim),
+        (((a_dim,), (b_dim,)), ((), ())),
+        preferred_element_type=jnp.float32,
+    )
+
+
+def product_f32(a, b, b_dim):
+    pairs = ((0, 0), (0, 1), (1, 0), (0, 2), (2, 0), (1, 1))
+    return lax.dot_general(
+        jnp.concatenate([a[p] for p, _ in pairs], axis=1),
+        jnp.concatenate([b[q] for _, q in pairs], axis=b_dim),
         (((1,), (b_dim,)), ((), ())),
         preferred_element_type=jnp.float32,
     )
@@ -95,7 +105,7 @@
     return jnp.concatenate(t, axis=0) if len(t) > 1 else t[0]
 
 
-def factor_step(m_ref, k, size, group):
+def factor_step(m_ref, k, size, group, always):
     n = m_ref.shape[0]
     active = k < n // size
     here = pl.ds(pl.multiple_of(jnp.minimum(k, n // size - 1) * size, size), size)
@@ -113,19 +123,21 @@
     inverse = pltpu.roll(t, 128 - size, 1)[:, :size]
     head = jnp.where(lane < size, jnp.where(lane == row, 1.0, 0.0), panel[:, :128])
     yield
-    done = dot_f32(inverse, jnp.concatenate([head, panel[:, 128:]], axis=1), 0)
+    done = dot_f32(inverse, jnp.concatenate([head, panel[:, 128:]], axis=1), 1, 0)
     yield
-    low = dot_f32(m_ref[:, :size], inverse, 1)
+    low = dot_f32(m_ref[:, :size], inverse, 1, 1)
     yield
     low = jnp.where(ids((n, size))[0] >= (k + 1) * size, low, 0.0)
-    change = dot_f32(low, done, 0)
+    change = dot_f32(low, done, 1, 0)
     for r in range(0, n, 32):
         yield
         full = m_ref[r : r + 32, :]
         new = jnp.where(ids((32, n))[1] < size, 0.0, full) - change[r : r + 32, :]
-        m_ref[r : r + 32, :] = jnp.where(active, pltpu.roll(new, n - size, 1), full)
+        new = pltpu.roll(new, n - size, 1)
+        m_ref[r : r + 32, :] = new if always else jnp.where(active, new, full)
     yield
-    m_ref[here, :] = jnp.where(active, pltpu.roll(done, n - size, 1), panel)
+    done = pltpu.roll(done, n - size, 1)
+    m_ref[here, :] = done if always else jnp.where(active, done, panel)
 
 
 def fill_phases(mine, parts_refs, sums_ref, pt_ref):
@@ -243,9 +255,10 @@
     rows, lead, cols, n_epoch, n_row = shape
     parts_refs, refs = refs[:n_epoch], refs[n_epoch:]
     held_refs, refs = refs[:n_row], refs[n_row:]
-    harmonic_ref, scale_ref, taps_ref, ridge_ref, panel_ref, schur_ref = refs[:6]
+    harmonic_ref, scale_ref, taps_ref, ridge_ref, panel_out, schur_out = refs[:6]
     sums_ref, pt_ref, wt_ref, dl_ref, lead_ref, block_ref = refs[6:12]
-    h_ref, r_ref, d_ref, fa_ref, fb_ref, acc_ref, m_ref, first_ref = refs[12:]
+    h_ref, r_ref, d_ref, fa_ref, fb_ref, acc_ref, m_ref, first_ref = refs[12:20]
+    panel_ref, schur_ref, sem = refs[20:]
     width, tile = fa_ref.shape
     count = wt_ref.shape[1]
     step = pl.program_id(0)
@@ -286,10 +299,16 @@
     def _():
         fill_phases(lax.axis_index("epoch"), parts_refs, sums_ref, pt_ref)
         fill_toeplitz(taps_ref, wt_ref)
-        r_ref[...] = parameter_table(harmonic_ref[...], scale_ref[...])
+        if rows % 128 or cols % 128:
+            r_ref[...] = parameter_table(harmonic_ref[...], scale_ref[...])
+            h_ref[:rows, :] = r_ref[pl.ds(first_row, rows), :]
+            h_ref[rows + lead :, :] = r_ref[pl.ds(first_col, cols), :]
+        else:
+            for at, first, size in ((0, first_row, rows), (rows + lead, first_col, cols)):
+                span = pl.ds(first, size)
+                h_ref[at : at + size, :] = parameter_table(harmonic_ref[:, span], scale_ref[:, span])
+            r_ref[:lead, :] = parameter_table(harmonic_ref[:, :lead], scale_ref[:, :lead])
         fill_lead(r_ref, pt_ref, wt_ref, dl_ref, lead_ref, block_ref)
-        h_ref[:rows, :] = r_ref[pl.ds(first_row, rows), :]
-        h_ref[rows + lead :, :] = r_ref[pl.ds(first_col, cols), :]
         acc_ref[...] = jnp.zeros_like(acc_ref)
         d_ref[...] = jnp.zeros_like(d_ref)
         first = []
@@ -341,7 +360,8 @@
             design(following, row)()
             next(extra, None)
 
-    factor = factor_step(m_ref, step, FACTOR_BLOCK, FACTOR_GROUP)
+    always = epochs // (2 * tile) <= lead // FACTOR_BLOCK
+    factor = factor_step(m_ref, step, FACTOR_BLOCK, FACTOR_GROUP, always)
     phase(fa_ref, 0, factor)
     phase(fb_ref, 1, factor)
     for _ in factor:
@@ -356,31 +376,39 @@
         own = jnp.concatenate([own, jnp.zeros((127, mid), jnp.float32)]).T[:rows, :1]
         first = first_ref[:, :1]
         scale = 1.0 / epochs
-        i = lax.broadcasted_iota(jnp.int32, (rows, lead + cols), 0) + first_row
-        j = lax.broadcasted_iota(jnp.int32, (rows, lead + cols), 1)
-        j = jnp.where(j < lead, j, j - lead + first_col)
-        acc_ref[:rows, :] = acc_ref[:rows, :] * scale + jnp.where(i == j, own, 0.0)
-        i = lax.broadcasted_iota(jnp.int32, (lead, cols), 0)
-        j = lax.broadcasted_iota(jnp.int32, (lead, cols), 1) + first_col
-        acc_ref[rows:, lead:] = acc_ref[rows:, lead:] * scale + jnp.where(i == j, first, 0.0)
+        @pl.loop(epochs // (2 * tile), max(lead // FACTOR_BLOCK, epochs // (2 * tile)))
+        def _(k):
+            for _ in factor_step(m_ref, k, FACTOR_BLOCK, FACTOR_GROUP, True):
+                pass
+
+        def total(begin, end, first, width_of, first_id, diagonal):
+            i = lax.broadcasted_iota(jnp.int32, (end - begin, width_of), 0)
+            j = lax.broadcasted_iota(jnp.int32, (end - begin, width_of), 1) + first_id
+            i = i + first_row if begin == 0 else i
+            block = acc_ref[begin:end, first : first + width_of]
+            return block * scale + jnp.where(i == j, diagonal, 0.0)
+
         i = lax.broadcasted_iota(jnp.int32, (lead, lead), 0)
         j = lax.broadcasted_iota(jnp.int32, (lead, lead), 1)
-
-        @pl.loop(epochs // (2 * tile), max(lead // FACTOR_BLOCK, epochs // (2 * tile)))
-        def _(k):
-            for _ in factor_step(m_ref, k, FACTOR_BLOCK, FACTOR_GROUP):
-                pass
-
-        inverse = jnp.where(i >= j, m_ref[...], 0.0)
-        highest = functools.partial(
-            lax.dot_general, precision=lax.Precision.HIGHEST, preferred_element_type=jnp.float32
-        )
-        panel_ref[...] = highest(acc_ref[:rows, :lead], inverse, (((1,), (1,)), ((), ())))
-        for c in range(0, cols, 256):
-            solved = highest(inverse, acc_ref[rows:, lead + c : lead + c + 256], (((1,), (0,)), ((), ())))
-            schur_ref[:, c : c + 256] = acc_ref[:rows, lead + c : lead + c + 256] - highest(
-                panel_ref[...], solved, (((1,), (0,)), ((), ()))
+        inverse = split3(jnp.where(i >= j, m_ref[...], 0.0))
+        panel = product_f32(split3(total(0, rows, 0, lead, 0, own)), inverse, 1)
+        panel_ref[...] = panel
+        copies = [pltpu.make_async_copy(panel_ref, panel_out, sem.at[0])]
+        copies[0].start()
+        panel = split3(panel)
+        for n, c in enumerate(range(0, cols, 256)):
+            size = min(256, cols - c)
+            span = slice(c, c + size)
+            right = total(rows, rows + lead, lead + c, size, first_col + c, first)
+            solved = split3(product_f32(inverse, split3(right), 0))
+            left = total(0, rows, lead + c, size, first_col + c, own)
+            schur_ref[:, span] = left - product_f32(panel, solved, 0)
+            copies.append(
+                pltpu.make_async_copy(schur_ref.at[:, span], schur_out.at[:, span], sem.at[n + 1])
             )
+            copies[-1].start()
+        for copy in copies:
+            copy.wait()
 
 
 def on_device(steps, harmonic, col_scale, taps, ridge):
@@ -397,7 +425,8 @@
     here = steps.shape[1]
     ridge_rows = -(-rows // here)
     ridge_part = jnp.pad(ridge, (0, ridge_rows * here - rows)).reshape(ridge_rows, here)
-    parts = rotated(jnp.concatenate([steps.astype(jnp.float32), ridge_part]), "epoch")
+    packed = jnp.pad(steps, ((0, ridge_rows), (0, 0))).astype(jnp.float32)
+    parts = rotated(packed + jnp.pad(ridge_part, ((2, 0), (0, 0))), "epoch")
     held = rotated(jnp.stack([x[2:, : min(rows, here)].reshape(-1) for x in parts]), "prow")
     row_of = lambda x: x.reshape(1, -1)
     in_vmem = pl.BlockSpec(memory_space=pltpu.VMEM)
@@ -409,7 +438,7 @@
         grid=(epochs // (2 * tile),),
         out_shape=(f32(rows, B), f32(rows, cols)),
         in_specs=[in_vmem] * len(operands),
-        out_specs=(in_vmem, in_vmem),
+        out_specs=(pl.BlockSpec(memory_space=pl.ANY),) * 2,
         scratch_shapes=[
             vmem(jnp.float32, 2 * epochs // 128, 128),
             vmem(jnp.float32, 8, epochs),
@@ -425,6 +454,9 @@
             vmem(jnp.float32, rows + B, B + cols),
             vmem(jnp.float32, B, B),
             vmem(jnp.float32, B, 128),
+            vmem(jnp.float32, rows, B),
+            vmem(jnp.float32, rows, cols),
+            pltpu.SemaphoreType.DMA((1 + -(-cols // 256),)),
         ],
         compiler_params=pltpu.CompilerParams(vmem_limit_bytes=VMEM_LIMIT),
     )(*operands)

time: 76.5 us -> 75.1 us (0.982)
  Pallas kernels: 59 us -> 57.6 us
    pallas_call x1, Pallas kernels: 59 us -> 57.6 us  [on_device(): pl.pallas_call(functools.partial(main_kernel, (rows, B, cols, n_epoch, n_...]
where the time goes in v6:
time: 75.1 us; the launch traced here: 74.8 us
  Pallas kernels  57.6 us (77%)
  starting transfers between devices  7.67 us (10%)
  waiting for transfers between devices  6.84 us (9%)
  local copies, waits for them, and re-layouts  1.28 us (2%)
    pallas_call x1, Pallas kernels, on_device(): pl.pallas_call(functools.partial(main_kernel, (rows, B, cols, n_epoch, n_...  57.6 us
    ppermute x4, starting transfers between devices, rotated(): return [x] + [lax.ppermute(x, axis, pairs) for pairs in shifts]  7.67 us
    ppermute x4, waiting for transfers between devices, rotated(): return [x] + [lax.ppermute(x, axis, pairs) for pairs in shifts]  6.84 us
  transfers between devices with their start and end apart: 4, of which 4 were waited for; matrix products, arithmetic and copies ran while one was open for 0% of the time, Pallas kernels for 0%

profile of v6, /device:TPU:0, one launch (start us, length us, event | category | flops | bytes accessed | tf_op | source)
XLA Modules:
  0.0 74.8 jit_solution(573300528034010493)
XLA Ops:
  0.6 0.7 pad.13
  1.3 0.7 pad_add_fusion.refs_0_
  2.1 0.0 copy-start
  2.1 5.1 %collective-permute-start.2 = (f32[3,2048]{1,0:T(4,128)S(1)}, f32[3,2048]{1,0:T(4,128)S(1)}, u32[]{:S(2)}, u32[]{:S(2)}) collective-permute-start(f32[3,2048]{1,0:T(4,128)S(1)} %pad_add_fusion.refs_0_), channel_id=1, source_target_pairs={{0,24},{8,0},{16,8},{24,16},{1,25},{9,1},{17,9},{25,17},{2,26},{10... | collective-permute-start | bytes 73736 | tf_op jit(solution)/shard_map/ppermute | solution.py:24
  7.2 0.0 collective-permute-start.1
  7.2 1.0 %collective-permute-start = (f32[3,2048]{1,0:T(4,128)S(1)}, f32[3,2048]{1,0:T(4,128)S(1)}, u32[]{:S(2)}, u32[]{:S(2)}) collective-permute-start(f32[3,2048]{1,0:T(4,128)S(1)} %pad_add_fusion.refs_0_), channel_id=1, source_target_pairs={{0,8},{8,16},{16,24},{24,0},{1,9},{9,17},{17,25},{25,1},{2,10},{10... | collective-permute-start | bytes 73736 | tf_op jit(solution)/shard_map/ppermute | solution.py:24
  8.2 0.6 collective-permute-done.2.refs_3_
  8.8 0.0 copy-start.1
  8.8 3.2 %collective-permute-done.1.refs_2_ = f32[3,2048]{1,0:T(4,128)S(1)} collective-permute-done((f32[3,2048]{1,0:T(4,128)S(1)}, f32[3,2048]{1,0:T(4,128)S(1)}, u32[]{:S(2)}, u32[]{:S(2)}) %collective-permute-start.1) | collective-permute-done | bytes 24608 | tf_op jit(solution)/shard_map/ppermute | solution.py:24
  12.0 0.0 copy-start.2
  12.0 0.9 %collective-permute-done.refs_1_ = f32[3,2048]{1,0:T(4,128)S(1)} collective-permute-done((f32[3,2048]{1,0:T(4,128)S(1)}, f32[3,2048]{1,0:T(4,128)S(1)}, u32[]{:S(2)}, u32[]{:S(2)}) %collective-permute-start) | collective-permute-done | bytes 24608 | tf_op jit(solution)/shard_map/ppermute | solution.py:24
  12.9 0.0 copy-start.3
  12.9 0.0 copy-start.4
  12.9 1.6 %collective-permute-start.3 = (f32[4,512]{1,0:T(4,128)S(1)}, f32[4,512]{1,0:T(4,128)S(1)}, u32[]{:S(2)}, u32[]{:S(2)}) collective-permute-start(f32[4,512]{1,0:T(4,128)S(1)} %pad_maximum_fusion.refs_4_), channel_id=1, source_target_pairs={{0,4},{4,0},{1,5},{5,1},{2,6},{6,2},{3,7},{7,3},{8,12},{12,8},{9,1... | collective-permute-start | bytes 24584 | tf_op jit(solution)/shard_map/ppermute | solution.py:24
  14.5 2.2 %collective-permute-done.3.refs_5_ = f32[4,512]{1,0:T(4,128)S(1)} collective-permute-done((f32[4,512]{1,0:T(4,128)S(1)}, f32[4,512]{1,0:T(4,128)S(1)}, u32[]{:S(2)}, u32[]{:S(2)}) %collective-permute-start.3) | collective-permute-done | bytes 8224 | tf_op jit(solution)/shard_map/ppermute | solution.py:24
  16.6 0.0 copy-start.5
  16.6 0.0 copy-done
  16.6 0.0 copy-done.1
  16.6 0.0 copy-done.2
  16.6 0.0 copy-done.3
  16.7 0.0 copy-done.4
  16.7 0.6 copy-done.5
  17.2 57.6 %shard_map.68 = (f32[512,256]{1,0:T(8,128)}, f32[512,1024]{1,0:T(8,128)}) custom-call(f32[3,2048]{1,0:T(4,128)} %copy-done, f32[3,2048]{1,0:T(4,128)} %copy-done.3, f32[3,2048]{1,0:T(4,128)} %copy-done.2, f32[3,2048]{1,0:T(4,128)} %copy-done.1, f32[4,512]{1,0:T(4,128)} %copy-done.4, f32[4,512]{1,0:T(4,128)} %copy-done.5, s32[1,4096]{1,0:T(1,128)} %bitcast.6, ...), custom_call_target="tpu_custom_call" | custom-call | tf_op jit(solution)/shard_map/pallas_call | solution.py:436
  (5 shorter events, 0.0 us)
Async XLA Ops:
  2.1 14.6 %copy-start = (f32[3,2048]{1,0:T(4,128)}, f32[3,2048]{1,0:T(4,128)S(1)}, u32[]{:S(2)}) copy-start(f32[3,2048]{1,0:T(4,128)S(1)} %pad_add_fusion.refs_0_) | copy-start | bytes 73732
  2.1 6.7 %collective-permute-start.2 = (f32[3,2048]{1,0:T(4,128)S(1)}, f32[3,2048]{1,0:T(4,128)S(1)}, u32[]{:S(2)}, u32[]{:S(2)}) collective-permute-start(f32[3,2048]{1,0:T(4,128)S(1)} %pad_add_fusion.refs_0_), channel_id=1, source_target_pairs={{0,24},{8,0},{16,8},{24,16},{1,25},{9,1},{17,9},{25,17},{2,26},{10... | collective-permute-start | bytes 73736 | tf_op jit(solution)/shard_map/ppermute | solution.py:24
  7.2 4.8 %collective-permute-start.1 = (f32[3,2048]{1,0:T(4,128)S(1)}, f32[3,2048]{1,0:T(4,128)S(1)}, u32[]{:S(2)}, u32[]{:S(2)}) collective-permute-start(f32[3,2048]{1,0:T(4,128)S(1)} %pad_add_fusion.refs_0_), channel_id=1, source_target_pairs={{0,16},{8,24},{16,0},{24,8},{1,17},{9,25},{17,1},{25,9},{2,18},{10... | collective-permute-start | bytes 73736 | tf_op jit(solution)/shard_map/ppermute | solution.py:24
  7.2 5.7 %collective-permute-start = (f32[3,2048]{1,0:T(4,128)S(1)}, f32[3,2048]{1,0:T(4,128)S(1)}, u32[]{:S(2)}, u32[]{:S(2)}) collective-permute-start(f32[3,2048]{1,0:T(4,128)S(1)} %pad_add_fusion.refs_0_), channel_id=1, source_target_pairs={{0,8},{8,16},{16,24},{24,0},{1,9},{9,17},{17,25},{25,1},{2,10},{10... | collective-permute-start | bytes 73736 | tf_op jit(solution)/shard_map/ppermute | solution.py:24
  8.8 7.9 %copy-start.1 = (f32[3,2048]{1,0:T(4,128)}, f32[3,2048]{1,0:T(4,128)S(1)}, u32[]{:S(2)}) copy-start(f32[3,2048]{1,0:T(4,128)S(1)} %collective-permute-done.2.refs_3_) | copy-start | bytes 73732
  12.0 4.7 %copy-start.2 = (f32[3,2048]{1,0:T(4,128)}, f32[3,2048]{1,0:T(4,128)S(1)}, u32[]{:S(2)}) copy-start(f32[3,2048]{1,0:T(4,128)S(1)} %collective-permute-done.1.refs_2_) | copy-start | bytes 73732
  12.9 3.8 %copy-start.3 = (f32[3,2048]{1,0:T(4,128)}, f32[3,2048]{1,0:T(4,128)S(1)}, u32[]{:S(2)}) copy-start(f32[3,2048]{1,0:T(4,128)S(1)} %collective-permute-done.refs_1_) | copy-start | bytes 73732
  12.9 3.8 %copy-start.4 = (f32[4,512]{1,0:T(4,128)}, f32[4,512]{1,0:T(4,128)S(1)}, u32[]{:S(2)}) copy-start(f32[4,512]{1,0:T(4,128)S(1)} %pad_maximum_fusion.refs_4_) | copy-start | bytes 24580
  12.9 3.7 %collective-permute-start.3 = (f32[4,512]{1,0:T(4,128)S(1)}, f32[4,512]{1,0:T(4,128)S(1)}, u32[]{:S(2)}, u32[]{:S(2)}) collective-permute-start(f32[4,512]{1,0:T(4,128)S(1)} %pad_maximum_fusion.refs_4_), channel_id=1, source_target_pairs={{0,4},{4,0},{1,5},{5,1},{2,6},{6,2},{3,7},{7,3},{8,12},{12,8},{9,1... | collective-permute-start | bytes 24584 | tf_op jit(solution)/shard_map/ppermute | solution.py:24
  16.6 0.6 copy-start.5

commit v7 on v6

--- a/solution.py
+++ b/solution.py
@@ -235,7 +235,7 @@
     for b in range(blocks):
         design(0, b)
 
-    @pl.loop(0, tiles)
+    @pl.loop(0, tiles, unroll=2 - tiles % 2)
     def _(step):
         following = pl.multiple_of(lax.rem((step + 1) * tile, epochs), tile)
         out_ref = lead_ref.at[step]
@@ -254,7 +254,6 @@
 def main_kernel(shape, *refs):
     rows, lead, cols, n_epoch, n_row = shape
     parts_refs, refs = refs[:n_epoch], refs[n_epoch:]
-    held_refs, refs = refs[:n_row], refs[n_row:]
     harmonic_ref, scale_ref, taps_ref, ridge_ref, panel_out, schur_out = refs[:6]
     sums_ref, pt_ref, wt_ref, dl_ref, lead_ref, block_ref = refs[6:12]
     h_ref, r_ref, d_ref, fa_ref, fb_ref, acc_ref, m_ref, first_ref = refs[12:20]
@@ -312,12 +311,18 @@
         acc_ref[...] = jnp.zeros_like(acc_ref)
         d_ref[...] = jnp.zeros_like(d_ref)
         first = []
+        local = parts_refs[0].shape[1]
+        deep = -(-rows // local)
         for q in range(-(-lead // rows)):
-            for k, ref in enumerate(held_refs):
-                group = lax.rem(lax.axis_index("prow") - k + n_row, n_row)
-                block = lax.rem(lax.axis_index("epoch") - q // n_row + n_epoch, n_epoch)
-                term = jnp.where(group == q % n_row, ref[pl.ds(block, 1), :rows], 0.0)
-                total = term if k == 0 else total + term
+            total = jnp.zeros((1, rows), jnp.float32)
+            for e, ref in enumerate(parts_refs):
+                for k in range(n_row):
+                    group = lax.rem(lax.axis_index("epoch") - e + n_epoch, n_epoch)
+                    row_group = lax.rem(lax.axis_index("prow") - k + n_row, n_row)
+                    held = [ref[2 + k * deep + d : 3 + k * deep + d, :] for d in range(deep)]
+                    held = jnp.concatenate(held, axis=1)[:, :rows]
+                    found = (group == q // n_row) & (row_group == q % n_row)
+                    total = total + jnp.where(found, held, 0.0)
             first.append(total)
         first = jnp.concatenate(first, axis=1)[:, :lead]
         first_ref[...] = jnp.concatenate([first, jnp.zeros((127, lead), jnp.float32)]).T
@@ -424,14 +429,15 @@
     tile = 512
     here = steps.shape[1]
     ridge_rows = -(-rows // here)
-    ridge_part = jnp.pad(ridge, (0, ridge_rows * here - rows)).reshape(ridge_rows, here)
-    packed = jnp.pad(steps, ((0, ridge_rows), (0, 0))).astype(jnp.float32)
-    parts = rotated(packed + jnp.pad(ridge_part, ((2, 0), (0, 0))), "epoch")
-    held = rotated(jnp.stack([x[2:, : min(rows, here)].reshape(-1) for x in parts]), "prow")
+    packed = jnp.pad(steps, ((0, n_row * ridge_rows), (0, 0))).astype(jnp.float32)
+    for k, x in enumerate(rotated(ridge, "prow")):
+        x = jnp.pad(x, (0, ridge_rows * here - rows)).reshape(ridge_rows, here)
+        packed = packed + jnp.pad(x, ((2 + k * ridge_rows, (n_row - 1 - k) * ridge_rows), (0, 0)))
+    parts = rotated(packed, "epoch")
     row_of = lambda x: x.reshape(1, -1)
     in_vmem = pl.BlockSpec(memory_space=pltpu.VMEM)
     f32 = lambda *shape: jax.ShapeDtypeStruct(shape, jnp.float32)
-    operands = (*parts, *held, row_of(harmonic), row_of(col_scale), row_of(taps), row_of(ridge))
+    operands = (*parts, row_of(harmonic), row_of(col_scale), row_of(taps), row_of(ridge))
     vmem = lambda dtype, *shape: pltpu.VMEM(shape, dtype)
     return pl.pallas_call(
         functools.partial(main_kernel, (rows, B, cols, n_epoch, n_row)),

time: 75.1 us -> 73.7 us (0.981)
  waiting for transfers between devices: 6.84 us -> 5.76 us
  Pallas kernels: 57.6 us -> 56.8 us
    ppermute x4, waiting for transfers between devices: 6.84 us -> 5.76 us  [rotated(): return [x] + [lax.ppermute(x, axis, pairs) for pairs in shifts]]
    pallas_call x1, Pallas kernels: 57.6 us -> 56.8 us  [on_device(): pl.pallas_call(functools.partial(main_kernel, (rows, B, cols, n_epoch, n_...]
  transfers between devices with their start and end apart: 4 -> 4, of which waited for: 4 -> 4; matrix products, arithmetic and copies ran while one was open for 0% -> 1% of each run, Pallas kernels for 0% -> 0%
where the time goes in v7:
time: 73.7 us; the launch traced here: 73.5 us
  Pallas kernels  56.8 us (77%)
  starting transfers between devices  8.2 us (11%)
  waiting for transfers between devices  5.76 us (8%)
  local copies, waits for them, and re-layouts  1.33 us (2%)
  other arithmetic  0.74 us (1%)
    pallas_call x1, Pallas kernels, on_device(): pl.pallas_call(functools.partial(main_kernel, (rows, B, cols, n_epoch, n_...  56.8 us
    ppermute x4, starting transfers between devices, rotated(): return [x] + [lax.ppermute(x, axis, pairs) for pairs in shifts]  8.2 us
    ppermute x4, waiting for transfers between devices, rotated(): return [x] + [lax.ppermute(x, axis, pairs) for pairs in shifts]  5.76 us
  transfers between devices with their start and end apart: 4, of which 4 were waited for; matrix products, arithmetic and copies ran while one was open for 1% of the time, Pallas kernels for 0%

profile of v7, /device:TPU:0, one launch (start us, length us, event | category | flops | bytes accessed | tf_op | source)
XLA Modules:
  0.0 73.5 jit_solution(14239033752082032235)
XLA Ops:
  0.6 3.0 %collective-permute-start = (f32[512]{0:T(512)}, f32[512]{0:T(512)S(1)}, u32[]{:S(2)}, u32[]{:S(2)}) collective-permute-start(f32[512]{0:T(512)} %param.9), channel_id=1, source_target_pairs={{0,4},{4,0},{1,5},{5,1},{2,6},{6,2},{3,7},{7,3},{8,12},{12,8},{9,1... | collective-permute-start | bytes 6152 | tf_op jit(solution)/shard_map/ppermute | solution.py:24
  3.6 0.7 pad.20
  4.4 1.1 %collective-permute-done = f32[512]{0:T(512)S(1)} collective-permute-done((f32[512]{0:T(512)}, f32[512]{0:T(512)S(1)}, u32[]{:S(2)}, u32[]{:S(2)}) %collective-permute-start) | collective-permute-done | bytes 2080 | tf_op jit(solution)/shard_map/ppermute | solution.py:24
  5.4 0.7 %pad_add_fusion.refs_0_ = f32[4,2048]{1,0:T(4,128)S(1)} fusion(f32[1,2048]{1,0:T(1,128)S(1)} %bitcast.7, f32[1,2048]{1,0:T(1,128)S(1)} %bitcast.6, s32[2,2048]{1,0:T(2,128)} %param.5), kind=kLoop, calls=%fused_computation | loop fusion | flops 24576 | bytes 65536 | tf_op jit(solution)/shard_map/add | solution.py:435
  6.2 0.0 copy-start
  6.2 4.2 %collective-permute-start.3 = (f32[4,2048]{1,0:T(4,128)S(1)}, f32[4,2048]{1,0:T(4,128)S(1)}, u32[]{:S(2)}, u32[]{:S(2)}) collective-permute-start(f32[4,2048]{1,0:T(4,128)S(1)} %pad_add_fusion.refs_0_), channel_id=1, source_target_pairs={{0,24},{8,0},{16,8},{24,16},{1,25},{9,1},{17,9},{25,17},{2,26},{10... | collective-permute-start | bytes 98312 | tf_op jit(solution)/shard_map/ppermute | solution.py:24
  10.3 0.0 collective-permute-start.2
  10.4 1.0 %collective-permute-start.1 = (f32[4,2048]{1,0:T(4,128)S(1)}, f32[4,2048]{1,0:T(4,128)S(1)}, u32[]{:S(2)}, u32[]{:S(2)}) collective-permute-start(f32[4,2048]{1,0:T(4,128)S(1)} %pad_add_fusion.refs_0_), channel_id=1, source_target_pairs={{0,8},{8,16},{16,24},{24,0},{1,9},{9,17},{17,25},{25,1},{2,10},{10... | collective-permute-start | bytes 98312 | tf_op jit(solution)/shard_map/ppermute | solution.py:24
  11.4 0.6 collective-permute-done.3.refs_3_
  11.9 0.0 copy-start.1
  12.0 3.2 %collective-permute-done.2.refs_2_ = f32[4,2048]{1,0:T(4,128)S(1)} collective-permute-done((f32[4,2048]{1,0:T(4,128)S(1)}, f32[4,2048]{1,0:T(4,128)S(1)}, u32[]{:S(2)}, u32[]{:S(2)}) %collective-permute-start.2) | collective-permute-done | bytes 32800 | tf_op jit(solution)/shard_map/ppermute | solution.py:24
  15.2 0.0 copy-start.2
  15.2 0.9 %collective-permute-done.1.refs_1_ = f32[4,2048]{1,0:T(4,128)S(1)} collective-permute-done((f32[4,2048]{1,0:T(4,128)S(1)}, f32[4,2048]{1,0:T(4,128)S(1)}, u32[]{:S(2)}, u32[]{:S(2)}) %collective-permute-start.1) | collective-permute-done | bytes 32800 | tf_op jit(solution)/shard_map/ppermute | solution.py:24
  16.1 0.0 copy-start.3
  16.1 0.0 copy-done
  16.1 0.0 copy-done.1
  16.1 0.0 copy-done.2
  16.1 0.6 copy-done.3
  16.7 56.8 %shard_map.68 = (f32[512,256]{1,0:T(8,128)}, f32[512,1024]{1,0:T(8,128)}) custom-call(f32[4,2048]{1,0:T(4,128)} %copy-done, f32[4,2048]{1,0:T(4,128)} %copy-done.3, f32[4,2048]{1,0:T(4,128)} %copy-done.2, f32[4,2048]{1,0:T(4,128)} %copy-done.1, s32[1,4096]{1,0:T(1,128)} %bitcast.8, f32[1,4096]{1,0:T(1,128)} %bitcast.9, f32[1,256]{1,0:T(1,128)} %bitcast.11, ...), custom_call_target="tpu_custom_call" | custom-call | tf_op jit(solution)/shard_map/pallas_call | solution.py:442
  (1 shorter events, 0.0 us)
Async XLA Ops:
  0.6 4.8 %collective-permute-start = (f32[512]{0:T(512)}, f32[512]{0:T(512)S(1)}, u32[]{:S(2)}, u32[]{:S(2)}) collective-permute-start(f32[512]{0:T(512)} %param.9), channel_id=1, source_target_pairs={{0,4},{4,0},{1,5},{5,1},{2,6},{6,2},{3,7},{7,3},{8,12},{12,8},{9,1... | collective-permute-start | bytes 6152 | tf_op jit(solution)/shard_map/ppermute | solution.py:24
  6.2 9.9 %copy-start = (f32[4,2048]{1,0:T(4,128)}, f32[4,2048]{1,0:T(4,128)S(1)}, u32[]{:S(2)}) copy-start(f32[4,2048]{1,0:T(4,128)S(1)} %pad_add_fusion.refs_0_) | copy-start | bytes 98308
  6.2 5.8 %collective-permute-start.3 = (f32[4,2048]{1,0:T(4,128)S(1)}, f32[4,2048]{1,0:T(4,128)S(1)}, u32[]{:S(2)}, u32[]{:S(2)}) collective-permute-start(f32[4,2048]{1,0:T(4,128)S(1)} %pad_add_fusion.refs_0_), channel_id=1, source_target_pairs={{0,24},{8,0},{16,8},{24,16},{1,25},{9,1},{17,9},{25,17},{2,26},{10... | collective-permute-start | bytes 98312 | tf_op jit(solution)/shard_map/ppermute | solution.py:24
  10.3 4.8 %collective-permute-start.2 = (f32[4,2048]{1,0:T(4,128)S(1)}, f32[4,2048]{1,0:T(4,128)S(1)}, u32[]{:S(2)}, u32[]{:S(2)}) collective-permute-start(f32[4,2048]{1,0:T(4,128)S(1)} %pad_add_fusion.refs_0_), channel_id=1, source_target_pairs={{0,16},{8,24},{16,0},{24,8},{1,17},{9,25},{17,1},{25,9},{2,18},{10... | collective-permute-start | bytes 98312 | tf_op jit(solution)/shard_map/ppermute | solution.py:24
  10.4 5.7 %collective-permute-start.1 = (f32[4,2048]{1,0:T(4,128)S(1)}, f32[4,2048]{1,0:T(4,128)S(1)}, u32[]{:S(2)}, u32[]{:S(2)}) collective-permute-start(f32[4,2048]{1,0:T(4,128)S(1)} %pad_add_fusion.refs_0_), channel_id=1, source_target_pairs={{0,8},{8,16},{16,24},{24,0},{1,9},{9,17},{17,25},{25,1},{2,10},{10... | collective-permute-start | bytes 98312 | tf_op jit(solution)/shard_map/ppermute | solution.py:24
  11.9 4.1 %copy-start.1 = (f32[4,2048]{1,0:T(4,128)}, f32[4,2048]{1,0:T(4,128)S(1)}, u32[]{:S(2)}) copy-start(f32[4,2048]{1,0:T(4,128)S(1)} %collective-permute-done.3.refs_3_) | copy-start | bytes 98308
  15.2 0.9 %copy-start.2 = (f32[4,2048]{1,0:T(4,128)}, f32[4,2048]{1,0:T(4,128)S(1)}, u32[]{:S(2)}) copy-start(f32[4,2048]{1,0:T(4,128)S(1)} %collective-permute-done.2.refs_2_) | copy-start | bytes 98308
  16.1 0.6 copy-start.3

commit v8 on v7

--- a/solution.py
+++ b/solution.py
@@ -15,7 +15,7 @@
 LEAD = SINE[3]
 POLY = tuple(c / LEAD for c in SINE[:3])
 VMEM_LIMIT = 58 * 1024 * 1024
-FACTOR_BLOCK, FACTOR_GROUP, FACTOR_SLAB = 32, 4, 32
+FACTOR_BLOCK, FACTOR_GROUP, FACTOR_SLAB = 32, 8, 8
 
 
 def rotated(x, axis):
@@ -244,11 +244,15 @@
             if b == min(1, blocks - 1):
                 d_ref[:, :count] = d_ref[:, tile:]
             if b > 0:
+                if b == blocks - 1:
+                    block_ref[...] += lax.dot_general(
+                        out_ref[...],
+                        out_ref[...],
+                        (((1,), (1,)), ((), ())),
+                        preferred_element_type=jnp.float32,
+                    )
                 design(following, b - 1)
         design(following, blocks - 1)
-        block_ref[...] += lax.dot_general(
-            out_ref[...], out_ref[...], (((1,), (1,)), ((), ())), preferred_element_type=jnp.float32
-        )
 
 
 def main_kernel(shape, *refs):

time: 73.7 us -> 73.5 us (level)
  no operation moved by 1% of the time
where the time goes in v8:
time: 73.5 us; the launch traced here: 73.3 us
  Pallas kernels  56.6 us (77%)
  starting transfers between devices  8.2 us (11%)
  waiting for transfers between devices  5.76 us (8%)
  local copies, waits for them, and re-layouts  1.33 us (2%)
  other arithmetic  0.74 us (1%)
    pallas_call x1, Pallas kernels, on_device(): pl.pallas_call(functools.partial(main_kernel, (rows, B, cols, n_epoch, n_...  56.6 us
    ppermute x4, starting transfers between devices, rotated(): return [x] + [lax.ppermute(x, axis, pairs) for pairs in shifts]  8.2 us
    ppermute x4, waiting for transfers between devices, rotated(): return [x] + [lax.ppermute(x, axis, pairs) for pairs in shifts]  5.76 us
  transfers between devices with their start and end apart: 4, of which 4 were waited for; matrix products, arithmetic and copies ran while one was open for 1% of the time, Pallas kernels for 0%

profile of v8, /device:TPU:0, one launch (start us, length us, event | category | flops | bytes accessed | tf_op | source)
XLA Modules:
  0.0 73.3 jit_solution(3382122574532792175)
XLA Ops:
  0.6 3.0 %collective-permute-start = (f32[512]{0:T(512)}, f32[512]{0:T(512)S(1)}, u32[]{:S(2)}, u32[]{:S(2)}) collective-permute-start(f32[512]{0:T(512)} %param.9), channel_id=1, source_target_pairs={{0,4},{4,0},{1,5},{5,1},{2,6},{6,2},{3,7},{7,3},{8,12},{12,8},{9,1... | collective-permute-start | bytes 6152 | tf_op jit(solution)/shard_map/ppermute | solution.py:24
  3.6 0.7 pad.20
  4.4 1.1 %collective-permute-done = f32[512]{0:T(512)S(1)} collective-permute-done((f32[512]{0:T(512)}, f32[512]{0:T(512)S(1)}, u32[]{:S(2)}, u32[]{:S(2)}) %collective-permute-start) | collective-permute-done | bytes 2080 | tf_op jit(solution)/shard_map/ppermute | solution.py:24
  5.4 0.7 %pad_add_fusion.refs_0_ = f32[4,2048]{1,0:T(4,128)S(1)} fusion(f32[1,2048]{1,0:T(1,128)S(1)} %bitcast.7, f32[1,2048]{1,0:T(1,128)S(1)} %bitcast.6, s32[2,2048]{1,0:T(2,128)} %param.5), kind=kLoop, calls=%fused_computation | loop fusion | flops 24576 | bytes 65536 | tf_op jit(solution)/shard_map/add | solution.py:439
  6.2 0.0 copy-start
  6.2 4.2 %collective-permute-start.3 = (f32[4,2048]{1,0:T(4,128)S(1)}, f32[4,2048]{1,0:T(4,128)S(1)}, u32[]{:S(2)}, u32[]{:S(2)}) collective-permute-start(f32[4,2048]{1,0:T(4,128)S(1)} %pad_add_fusion.refs_0_), channel_id=1, source_target_pairs={{0,24},{8,0},{16,8},{24,16},{1,25},{9,1},{17,9},{25,17},{2,26},{10... | collective-permute-start | bytes 98312 | tf_op jit(solution)/shard_map/ppermute | solution.py:24
  10.3 0.0 collective-permute-start.2
  10.4 1.0 %collective-permute-start.1 = (f32[4,2048]{1,0:T(4,128)S(1)}, f32[4,2048]{1,0:T(4,128)S(1)}, u32[]{:S(2)}, u32[]{:S(2)}) collective-permute-start(f32[4,2048]{1,0:T(4,128)S(1)} %pad_add_fusion.refs_0_), channel_id=1, source_target_pairs={{0,8},{8,16},{16,24},{24,0},{1,9},{9,17},{17,25},{25,1},{2,10},{10... | collective-permute-start | bytes 98312 | tf_op jit(solution)/shard_map/ppermute | solution.py:24
  11.4 0.6 collective-permute-done.3.refs_3_
  11.9 0.0 copy-start.1
  12.0 3.2 %collective-permute-done.2.refs_2_ = f32[4,2048]{1,0:T(4,128)S(1)} collective-permute-done((f32[4,2048]{1,0:T(4,128)S(1)}, f32[4,2048]{1,0:T(4,128)S(1)}, u32[]{:S(2)}, u32[]{:S(2)}) %collective-permute-start.2) | collective-permute-done | bytes 32800 | tf_op jit(solution)/shard_map/ppermute | solution.py:24
  15.2 0.0 copy-start.2
  15.2 0.9 %collective-permute-done.1.refs_1_ = f32[4,2048]{1,0:T(4,128)S(1)} collective-permute-done((f32[4,2048]{1,0:T(4,128)S(1)}, f32[4,2048]{1,0:T(4,128)S(1)}, u32[]{:S(2)}, u32[]{:S(2)}) %collective-permute-start.1) | collective-permute-done | bytes 32800 | tf_op jit(solution)/shard_map/ppermute | solution.py:24
  16.1 0.0 copy-start.3
  16.1 0.0 copy-done
  16.1 0.0 copy-done.1
  16.1 0.0 copy-done.2
  16.1 0.6 copy-done.3
  16.7 56.6 %shard_map.68 = (f32[512,256]{1,0:T(8,128)}, f32[512,1024]{1,0:T(8,128)}) custom-call(f32[4,2048]{1,0:T(4,128)} %copy-done, f32[4,2048]{1,0:T(4,128)} %copy-done.3, f32[4,2048]{1,0:T(4,128)} %copy-done.2, f32[4,2048]{1,0:T(4,128)} %copy-done.1, s32[1,4096]{1,0:T(1,128)} %bitcast.8, f32[1,4096]{1,0:T(1,128)} %bitcast.9, f32[1,256]{1,0:T(1,128)} %bitcast.11, ...), custom_call_target="tpu_custom_call" | custom-call | tf_op jit(solution)/shard_map/pallas_call | solution.py:446
  (1 shorter events, 0.0 us)
Async XLA Ops:
  0.6 4.8 %collective-permute-start = (f32[512]{0:T(512)}, f32[512]{0:T(512)S(1)}, u32[]{:S(2)}, u32[]{:S(2)}) collective-permute-start(f32[512]{0:T(512)} %param.9), channel_id=1, source_target_pairs={{0,4},{4,0},{1,5},{5,1},{2,6},{6,2},{3,7},{7,3},{8,12},{12,8},{9,1... | collective-permute-start | bytes 6152 | tf_op jit(solution)/shard_map/ppermute | solution.py:24
  6.2 9.9 %copy-start = (f32[4,2048]{1,0:T(4,128)}, f32[4,2048]{1,0:T(4,128)S(1)}, u32[]{:S(2)}) copy-start(f32[4,2048]{1,0:T(4,128)S(1)} %pad_add_fusion.refs_0_) | copy-start | bytes 98308
  6.2 5.8 %collective-permute-start.3 = (f32[4,2048]{1,0:T(4,128)S(1)}, f32[4,2048]{1,0:T(4,128)S(1)}, u32[]{:S(2)}, u32[]{:S(2)}) collective-permute-start(f32[4,2048]{1,0:T(4,128)S(1)} %pad_add_fusion.refs_0_), channel_id=1, source_target_pairs={{0,24},{8,0},{16,8},{24,16},{1,25},{9,1},{17,9},{25,17},{2,26},{10... | collective-permute-start | bytes 98312 | tf_op jit(solution)/shard_map/ppermute | solution.py:24
  10.3 4.8 %collective-permute-start.2 = (f32[4,2048]{1,0:T(4,128)S(1)}, f32[4,2048]{1,0:T(4,128)S(1)}, u32[]{:S(2)}, u32[]{:S(2)}) collective-permute-start(f32[4,2048]{1,0:T(4,128)S(1)} %pad_add_fusion.refs_0_), channel_id=1, source_target_pairs={{0,16},{8,24},{16,0},{24,8},{1,17},{9,25},{17,1},{25,9},{2,18},{10... | collective-permute-start | bytes 98312 | tf_op jit(solution)/shard_map/ppermute | solution.py:24
  10.4 5.7 %collective-permute-start.1 = (f32[4,2048]{1,0:T(4,128)S(1)}, f32[4,2048]{1,0:T(4,128)S(1)}, u32[]{:S(2)}, u32[]{:S(2)}) collective-permute-start(f32[4,2048]{1,0:T(4,128)S(1)} %pad_add_fusion.refs_0_), channel_id=1, source_target_pairs={{0,8},{8,16},{16,24},{24,0},{1,9},{9,17},{17,25},{25,1},{2,10},{10... | collective-permute-start | bytes 98312 | tf_op jit(solution)/shard_map/ppermute | solution.py:24
  11.9 4.1 %copy-start.1 = (f32[4,2048]{1,0:T(4,128)}, f32[4,2048]{1,0:T(4,128)S(1)}, u32[]{:S(2)}) copy-start(f32[4,2048]{1,0:T(4,128)S(1)} %collective-permute-done.3.refs_3_) | copy-start | bytes 98308
  15.2 0.9 %copy-start.2 = (f32[4,2048]{1,0:T(4,128)}, f32[4,2048]{1,0:T(4,128)S(1)}, u32[]{:S(2)}) copy-start(f32[4,2048]{1,0:T(4,128)S(1)} %collective-permute-done.2.refs_2_) | copy-start | bytes 98308
  16.1 0.6 copy-start.3
